TPU v7x, 32 devices: a whole 2x2x4 slice. The times are simulated.
32 devices in a mesh: dp: 8 (over y, x, core), mp: 4 (over z).
Axes of the slice: x: 2, y: 2, z: 4, core: 2. Of those that a mesh axis runs over, the one named last changes fastest.
Arguments:
- queries: bfloat16 [1024, 4096], P('dp', 'mp'), may hold values from -100 to 100
- neighbours: bfloat16 [128, 64, 896], P(None, 'dp'), may hold values from -6 to 6
- targets: int32 [64], P('dp'), may hold values from 0 to 31, as said below
- counts: int32 [8], P('dp'), may hold values from 0 to 8, as said below
- in_weight: bfloat16 [896, 3584], P(None, 'mp'), may hold values from -0.1875 to 0.1875
- out_weight: bfloat16 [3584, 896], P('mp'), may hold values from -0.09375 to 0.09375
- kv_weight: bfloat16 [896, 2, 4096], P(None, None, 'mp'), may hold values from -0.1875 to 0.1875
- d_context: bfloat16 [1024, 4096], P('dp', 'mp'), may hold values from -6 to 6
Outputs:
- context: bfloat16 [1024, 4096], P('dp', 'mp')
- d_queries: bfloat16 [1024, 4096], P('dp', 'mp')
- grad_kv: float32 [896, 2, 4096], P('dp', None, 'mp')
- grad_in: float32 [896, 3584], P('dp', 'mp')
- grad_out: float32 [3584, 896], P('mp', 'dp')
Inputs may be any that keep to these rules, and one draw needn't show every extreme that they name: Every block index o * 4 + p (o an owner, p < 4) is the target of exactly one live slot over all holders; at most 1 live slots of one holder target one owner, and some holder reaches 1; targets of slots that are not live are arbitrary. counts sum to 4 times the number of devices along dp.
All inputs are finite; a program needn't handle non-finite values.
Results may differ from a plain program's by a relative error of at most 0.04.
Values may be sent and summed in bfloat16 or wider, within the bound.
A program may use at most 64 MiB of HBM per device.

v0:
```python
import jax
import jax.numpy as jnp
from jax import lax
from jax.sharding import PartitionSpec as P

DH = 128
SPAN = 64
NEIGH = 2


GELU_C = 0.7978845608028654
GELU_A = 0.044715
EPSILON = 1e-06


def gelu_value(values):
    inner = GELU_C * (values + GELU_A * values * values * values)
    return 0.5 * values * (1.0 + jnp.tanh(inner))


def gelu_slope(values):
    inner = GELU_C * (values + GELU_A * values * values * values)
    tanh_value = jnp.tanh(inner)
    return 0.5 * (1.0 + tanh_value) + 0.5 * values * (1.0 - tanh_value * tanh_value) * GELU_C * (
        1.0 + 3.0 * GELU_A * values * values
    )


def rms_normed(rows):
    wide = rows.astype(jnp.float32)
    mean_square = jnp.mean(wide * wide, axis=-1, keepdims=True)
    return (wide * lax.rsqrt(mean_square + EPSILON)).astype(jnp.bfloat16)


def encode_front(rows, in_weight):
    length, spread, columns = rows.shape
    normed = rms_normed(rows).reshape(length * spread, columns)
    hidden_pre = jnp.dot(normed, in_weight, preferred_element_type=jnp.float32)
    activated = gelu_value(hidden_pre).astype(jnp.bfloat16)
    return (normed, hidden_pre, activated)


def to_spans(values, spans):
    length, blocks, columns = values.shape
    heads = columns // DH
    return (
        values.reshape(length, spans, 2, heads, DH)
        .transpose(1, 2, 0, 3, 4)
        .reshape(spans, 2 * length, heads, DH)
    )


def from_spans(values, length):
    spans, keys_len, heads, depth = values.shape
    return (
        values.reshape(spans, 2, length, heads, depth)
        .transpose(2, 0, 1, 3, 4)
        .reshape(length, 2 * spans, heads * depth)
    )


def attend(queries, keys, values, grads):
    scaling = DH ** (-0.5)
    scores = (
        jnp.einsum("cqhd,ckhd->chqk", queries, keys, preferred_element_type=jnp.float32) * scaling
    )
    peak = jnp.max(scores, axis=-1, keepdims=True)
    weights = jnp.exp(scores - peak)
    probs_wide = weights / jnp.sum(weights, axis=-1, keepdims=True)
    probs = probs_wide.astype(jnp.bfloat16)
    context = jnp.einsum(
        "chqk,ckhd->cqhd", probs, values, preferred_element_type=jnp.float32
    ).astype(jnp.bfloat16)
    d_probs = jnp.einsum("cqhd,ckhd->chqk", grads, values, preferred_element_type=jnp.float32)
    d_scores = (
        probs_wide * (d_probs - jnp.sum(d_probs * probs_wide, axis=-1, keepdims=True)) * scaling
    ).astype(jnp.bfloat16)
    d_queries = jnp.einsum(
        "chqk,ckhd->cqhd", d_scores, keys, preferred_element_type=jnp.float32
    ).astype(jnp.bfloat16)
    d_keys = jnp.einsum(
        "chqk,cqhd->ckhd", d_scores, queries, preferred_element_type=jnp.float32
    ).astype(jnp.bfloat16)
    d_values = jnp.einsum(
        "chqk,cqhd->ckhd", probs, grads, preferred_element_type=jnp.float32
    ).astype(jnp.bfloat16)
    return (context, d_queries, d_keys, d_values)


def per_device(queries, neighbours, targets, counts, in_weight, out_weight, kv_weight, d_context):
    length, holding, enc_width = neighbours.shape
    devices_dp = lax.axis_size("dp")
    devices_mp = lax.axis_size("mp")
    slice_rows = length // devices_mp
    token_rows, local_columns = queries.shape
    spans = token_rows // SPAN
    blocks = NEIGH * spans
    capacity = max(1, 2 * blocks // devices_dp)
    my_rank = lax.axis_index("mp")
    slot_ids = jnp.arange(holding, dtype=jnp.int32)
    is_live = slot_ids < counts[0]
    dest_owner = targets // blocks
    slot_place = targets % blocks
    owner_hits = jnp.logical_and(
        dest_owner[:, None] == jnp.arange(devices_dp, dtype=jnp.int32)[None, :], is_live[:, None]
    ).astype(jnp.int32)
    earlier = jnp.cumsum(owner_hits, axis=0) - owner_hits
    ranking = jnp.sum(earlier * owner_hits, axis=1)
    dest_slot = jnp.where(is_live, dest_owner * capacity + ranking, -1)
    selector_ints = (
        jnp.arange(devices_dp * capacity, dtype=jnp.int32)[:, None] == dest_slot[None, :]
    ).astype(jnp.int32)
    selector = selector_ints.astype(jnp.bfloat16)
    filled = jnp.sum(selector_ints, axis=1) > 0
    sent_place = jnp.where(filled, jnp.sum(selector_ints * slot_place[None, :], axis=1), -1)
    sent_place = sent_place.reshape(1, devices_dp, capacity, 1)
    own_slice = lax.dynamic_slice_in_dim(neighbours, my_rank * slice_rows, slice_rows, 0)
    normed, hidden_pre, activated = encode_front(neighbours, in_weight)
    picked = activated
    summed = lax.psum_scatter(
        jnp.dot(picked, out_weight, preferred_element_type=jnp.float32)
        .reshape(slice_rows * lax.axis_size("mp"), holding, enc_width)
        .astype(jnp.bfloat16),
        "mp",
        scatter_dimension=0,
        tiled=True,
    ).astype(jnp.float32)
    encoded = (own_slice.astype(jnp.float32) + summed).astype(jnp.bfloat16)
    moved = jnp.einsum("kh,thd->tkd", selector, encoded, preferred_element_type=jnp.float32).astype(
        jnp.bfloat16
    )
    received = lax.all_to_all(
        moved.reshape(slice_rows, devices_dp, capacity, enc_width),
        "dp",
        split_axis=1,
        concat_axis=1,
        tiled=True,
    )
    received_place = lax.all_to_all(sent_place, "dp", split_axis=1, concat_axis=1, tiled=True)
    placing = (
        received_place.reshape(1, -1) == jnp.arange(blocks, dtype=jnp.int32)[:, None]
    ).astype(jnp.bfloat16)
    rows = jnp.einsum(
        "bk,tkd->tbd",
        placing,
        received.reshape(slice_rows, -1, enc_width),
        preferred_element_type=jnp.float32,
    )
    slices, placing = (rows.astype(jnp.bfloat16), placing)
    piece = lax.all_gather(slices, "mp", axis=0, tiled=True)
    projected = jnp.einsum(
        "tbe,ejx->tbjx", piece, kv_weight, preferred_element_type=jnp.float32
    ).astype(jnp.bfloat16)
    gathered = piece
    heads = local_columns // DH
    heads_queries = queries.reshape(spans, SPAN, heads, DH)
    heads_grads = d_context.reshape(spans, SPAN, heads, DH)
    context, d_queries, d_keys, d_values = attend(
        heads_queries,
        to_spans(projected[:, :, 0], spans),
        to_spans(projected[:, :, 1], spans),
        heads_grads,
    )
    d_keyvals = jnp.stack([from_spans(d_keys, length), from_spans(d_values, length)], axis=2)
    picked = d_keyvals
    d_slices = lax.psum_scatter(
        jnp.einsum("tbjx,ejx->tbe", picked, kv_weight, preferred_element_type=jnp.float32).astype(
            jnp.bfloat16
        ),
        "mp",
        scatter_dimension=0,
        tiled=True,
    )
    kv_terms = jnp.einsum("tbe,tbjx->ejx", gathered, d_keyvals, preferred_element_type=jnp.float32)
    grad_kv = lax.psum_scatter(
        kv_terms.astype(jnp.bfloat16), "dp", scatter_dimension=0, tiled=True
    ).astype(jnp.float32)
    returned = jnp.einsum(
        "bk,tbd->tkd", placing, d_slices, preferred_element_type=jnp.float32
    ).astype(jnp.bfloat16)
    returned = returned.reshape(slice_rows, devices_dp, capacity, enc_width)
    back_home = lax.all_to_all(returned, "dp", split_axis=1, concat_axis=1, tiled=True)
    slot_grads = jnp.einsum(
        "kh,tkd->thd",
        selector,
        back_home.reshape(slice_rows, -1, enc_width),
        preferred_element_type=jnp.float32,
    ).astype(jnp.bfloat16)
    piece = lax.all_gather(slot_grads, "mp", axis=0, tiled=True)
    count = piece.shape[0]
    spread = piece.shape[1]
    flat = piece.reshape(count * spread, enc_width)
    d_act = jnp.einsum("ne,fe->nf", flat, out_weight, preferred_element_type=jnp.float32)
    d_pre = (d_act * gelu_slope(hidden_pre)).astype(jnp.bfloat16)
    in_total = jnp.einsum("ne,nf->ef", normed, d_pre, preferred_element_type=jnp.float32)
    out_total = jnp.einsum("ne,nf->ef", flat, activated, preferred_element_type=jnp.float32)
    in_total, out_total = (in_total, out_total)
    grad_in, grad_out_t = (
        lax.psum_scatter(
            in_total.astype(jnp.bfloat16), "dp", scatter_dimension=0, tiled=True
        ).astype(jnp.float32),
        lax.psum_scatter(
            out_total.astype(jnp.bfloat16), "dp", scatter_dimension=0, tiled=True
        ).astype(jnp.float32),
    )
    return (
        context.reshape(token_rows, local_columns),
        d_queries.reshape(token_rows, local_columns),
        grad_kv,
        grad_in,
        grad_out_t.T,
    )


def solution(mesh):
    placed = (
        P("dp", "mp"),
        P(None, "dp", None),
        P("dp"),
        P("dp"),
        P(None, "mp"),
        P("mp", None),
        P(None, None, "mp"),
        P("dp", "mp"),
    )
    return jax.shard_map(
        per_device,
        mesh=mesh,
        in_specs=placed,
        out_specs=(P("dp", "mp"), P("dp", "mp"), P("dp", None, "mp"), P("dp", "mp"), P("mp", "dp")),
        check_vma=False,
    )
```

profile of v0, /device:TPU:0, one launch (start us, length us, event | category | flops | bytes accessed | tf_op | source)
XLA Modules:
  0.0 385.4 jit_solution(4734310244268043453)
XLA Ops:
  7.2 2.0 fusion.2
  9.4 4.3 %fusion.27 = f32[1024,896]{1,0:T(8,128)S(1)} fusion(bf16[896,896]{1,0:T(8,128)(2,1)} %param.12, bf16[128,8,896]{2,1,0:T(8,128)(2,1)} %param.9, f32[128,8]{1,0:T(8,128)S(1)} %copy.109), kind=kOutput, calls=%fused_computation.31 | convolution fusion | flops 1646919680 | bytes 7114752 | tf_op jit(solution)/shard_map/dot_general | solution.py:38
  13.8 1.8 copy-done.8
  15.6 3.7 convert_bitcast_fusion
  21.0 5.2 %all-to-all-start.1 = ((s32[1,8,1,1]{3,2,0,1:T(1,128)}), s32[1,8,1,1]{3,2,0,1:T(1,128)S(1)}, u32[]{:S(2)}, u32[]{:S(2)}) async-start(s32[1,8,1,1]{3,2,0,1:T(1,128)} %copy.113), calls=%async_computation.2 | async-start | bytes 8192 | tf_op jit(solution)/shard_map/all_to_all | solution.py:139
  26.2 35.5 %reduce-scatter.5.cloned.1.call-done = bf16[32,8,896]{2,1,0:T(8,128)(2,1)} async-done(((bf16[128,8,896]{2,1,0:T(8,128)(2,1)}), bf16[32,8,896]{2,1,0:T(8,128)(2,1)}) %reduce-scatter.5.cloned.1.call-update) | async-done | bytes 458768 | tf_op jit(solution)/shard_map/reduce_scatter | solution.py:120
  64.0 3.6 all-to-all-start
  68.1 8.6 %all-to-all-done = bf16[32,8,1,896]{3,0,2,1:T(8,128)(2,1)S(1)} async-done(((bf16[32,8,1,896]{3,0,2,1:T(8,128)(2,1)}), bf16[32,8,1,896]{3,0,2,1:T(8,128)(2,1)S(1)}, u32[]{:S(2)}, u32[]{:S(2)}) %all-to-all-start) | async-done | bytes 458784 | tf_op jit(solution)/shard_map/all_to_all | solution.py:132
  77.0 19.2 %all_gather.6 = bf16[128,4,896]{2,1,0:T(4,128)(2,1)S(1)} all-gather(bf16[32,4,896]{2,1,0:T(4,128)(2,1)S(1)} %fusion.43), channel_id=1, replica_groups=mesh['dp'=8,'mp'=4] {'mp'}, dimensions={0}, use_global_device_ids=true | all-gather | bytes 1146880 | tf_op jit(solution)/shard_map/all_gather | solution.py:150
  96.2 4.8 %fusion.16 = bf16[128,4,2,1024]{3,0,2,1:T(8,128)(2,1)S(1)} fusion(bf16[896,2,1024]{2,1,0:T(2,128)(2,1)} %param.14, bf16[128,4,896,1]{2,1,0,3:T(4,128)(2,1)S(1)} %bitcast.153), kind=kOutput, calls=%fused_computation.22 | convolution fusion | flops 1880096768 | bytes 6684672 | tf_op jit(solution)/shard_map/tbe,ejx->tbjx/dot_general | solution.py:151
  105.6 4.8 %convolution_convert_fusion.1 = bf16[2,8,256,128]{3,2,1,0:T(8,128)(2,1)} fusion(bf16[2,64,8,128]{3,2,1,0:T(8,128)(2,1)S(1)} %bitcast.148, f32[2,8,64]{2,1,0:T(8,128)S(1)} %get-tuple-element.41, f32[2,8,64,256]{3,2,1,0:T(8,128)} %copy-done.2), kind=kOutput, calls=%fused_computation.33 | convolution fusion | flops 68420864 | bytes 2363392 | tf_op jit(solution)/shard_map/chqk,cqhd->ckhd/dot_general | solution.py:84
  110.4 9.3 %convolution_convert_fusion.2 = bf16[2,8,256,128]{3,2,1,0:T(8,128)(2,1)} fusion(f32[2,8,64,256]{3,2,1,0:T(8,128)} %convolution_bitcast_fusion, bf16[2,64,8,128]{3,2,1,0:T(8,128)(2,1)S(1)} %bitcast.146, f32[2,8,64,256]{3,2,1,0:T(8,128)} %get-tuple-element.42, f32[2,8,64]{2,1,0:T(8,128)S(1)} %get-tuple-element.41), kind=kOutput, calls=%fused_computation.34 | convolution fusion | flops 69469440 | bytes 3411968 | tf_op jit(solution)/shard_map/chqk,cqhd->ckhd/dot_general | solution.py:81
  119.7 2.9 copy.123
  122.6 2.3 stack_reshape.6
  124.9 2.3 constant_dynamic-update-slice_fusion.1
  127.2 2.9 copy.125
  130.1 2.3 stack_reshape.7
  132.3 2.4 constant_dynamic-update-slice_fusion
  134.7 5.1 %bitcast_convert_fusion.1 = bf16[128,4,896]{2,0,1:T(8,128)(2,1)S(1)} fusion(bf16[128,4,2,1024]{3,0,1,2:T(8,128)(2,1)} %constant_dynamic-update-slice_fusion, bf16[896,2,1024,1]{2,1,0,3:T(2,128)(2,1)} %bitcast.156), kind=kOutput, calls=%fused_computation.27 | convolution fusion | flops 1879506944 | bytes 6684672 | tf_op jit(solution)/shard_map/tbjx,ejx->tbe/dot_general | solution.py:167
  142.8 44.7 %all-reduce.3.cloned.1.call-done = bf16[128,4,896]{2,1,0:T(4,128)(2,1)} async-done(((bf16[128,4,896]{2,1,0:T(4,128)(2,1)}), bf16[128,4,896]{2,1,0:T(4,128)(2,1)}) %all-reduce.3.cloned.1.call-update) | async-done | bytes 917520
  188.8 12.5 %all_to_all.15 = bf16[32,8,1,896]{3,0,2,1:T(8,128)(2,1)S(1)} all-to-all(bf16[32,8,1,896]{3,0,2,1:T(8,128)(2,1)S(1)} %copy.129), channel_id=1, replica_groups=mesh['dp'=8,'mp'=4] {'dp'}, dimensions={1} | all-to-all | bytes 917504 | tf_op jit(solution)/shard_map/all_to_all | solution.py:182
  202.4 5.8 %bitcast_convert_fusion = bf16[896,2,1024]{2,0,1:T(8,128)(2,1)} fusion(bf16[128,4,2,1024]{3,0,1,2:T(8,128)(2,1)} %constant_dynamic-update-slice_fusion, bf16[128,4,896]{2,1,0:T(4,128)(2,1)} %copy-done.3), kind=kOutput, calls=%fused_computation.2 | convolution fusion | flops 1880883200 | bytes 6684672 | tf_op jit(solution)/shard_map/tbe,tbjx->ejx/dot_general | solution.py:174
  208.3 33.0 %all-gather.2.cloned.1.call-done = bf16[128,8,896]{2,1,0:T(8,128)(2,1)} async-done(((bf16[32,8,896]{2,1,0:T(8,128)(2,1)}), bf16[128,8,896]{2,1,0:T(8,128)(2,1)}) %all-gather.2.cloned.1.call-update) | async-done | bytes 1835024 | tf_op jit(solution)/shard_map/all_gather | solution.py:189
  241.4 9.4 %convolution_convert_fusion = bf16[896,896]{1,0:T(8,128)(2,1)} fusion(bf16[128,8,896]{2,1,0:T(8,128)(2,1)} %param.9, f32[128,8]{1,0:T(8,128)S(1)} %copy.109, f32[1024,896]{1,0:T(8,128)} %copy-done.8, bf16[896,896]{1,0:T(8,128)(2,1)S(1)} %copy-done, bf16[128,8,896]{2,1,0:T(8,128)(2,1)} %all-gather.2.cloned.1.call-done), kind=kOutput, calls=%fused_computation.30 | convolution fusion | flops 3309322240 | bytes 10555392 | tf_op jit(solution)/shard_map/ne,nf->ef/dot_general | solution.py:195
  251.1 6.5 %fusion.23 = bf16[896,896]{1,0:T(8,128)(2,1)} fusion(bf16[128,8,896]{2,1,0:T(8,128)(2,1)} %all-gather.2.cloned.1.call-done, f32[1024,896]{1,0:T(8,128)} %copy-done.8), kind=kOutput, calls=%fused_computation.29 | convolution fusion | flops 1653227520 | bytes 7110656 | tf_op jit(solution)/shard_map/ne,nf->ef/dot_general | solution.py:196
  257.6 7.9 %fusion.42 = bf16[2,64,8,128]{3,1,2,0:T(8,128)(2,1)S(1)} fusion(bf16[2,256,8,128]{3,1,2,0:T(8,128)(2,1)} %bitcast.140, f32[2,8,64,256]{3,2,1,0:T(8,128)} %convolution_bitcast_fusion, f32[2,8,64,256]{3,2,1,0:T(8,128)} %get-tuple-element.42, f32[2,8,64]{2,1,0:T(8,128)S(1)} %get-tuple-element.41), kind=kOutput, calls=%fused_computation.53 | convolution fusion | flops 69076224 | bytes 3411968 | tf_op jit(solution)/shard_map/chqk,ckhd->cqhd/dot_general | solution.py:78
  265.7 3.4 fusion.41
  270.2 22.1 %reduce-scatter.7.cloned.1.call-done = bf16[112,2,1024]{2,0,1:T(8,128)(2,1)} async-done(((bf16[896,2,1024]{2,0,1:T(8,128)(2,1)}), bf16[112,2,1024]{2,0,1:T(8,128)(2,1)}) %reduce-scatter.7.cloned.1.call-update) | async-done | bytes 458768 | tf_op jit(solution)/shard_map/reduce_scatter | solution.py:175
  292.3 2.4 copy.131
  294.7 40.1 %reduce-scatter.9.cloned.1.call-done = bf16[112,896]{1,0:T(8,128)(2,1)} async-done(((bf16[896,896]{1,0:T(8,128)(2,1)}), bf16[112,896]{1,0:T(8,128)(2,1)}) %reduce-scatter.9.cloned.1.call-update) | async-done | bytes 200720 | tf_op jit(solution)/shard_map/reduce_scatter | solution.py:199
  334.8 1.7 convert_element_type.148
  336.5 40.4 %reduce-scatter.11.cloned.1.call-done = bf16[112,896]{1,0:T(8,128)(2,1)} async-done(((bf16[896,896]{1,0:T(8,128)(2,1)}), bf16[112,896]{1,0:T(8,128)(2,1)}) %reduce-scatter.11.cloned.1.call-update) | async-done | bytes 200720 | tf_op jit(solution)/shard_map/reduce_scatter | solution.py:202
  (65 shorter events, 16.8 us)
Async XLA Ops:
  7.2 8.4 %copy-start = (bf16[896,896]{1,0:T(8,128)(2,1)S(1)}, bf16[896,896]{1,0:T(8,128)(2,1)}, u32[]{:S(2)}) copy-start(bf16[896,896]{1,0:T(8,128)(2,1)} %param.13) | copy-start | bytes 4816900
  7.2 54.5 %reduce-scatter.5.cloned.1.call-start = ((), (), s32[]{:S(2)}) async-start(), calls=%async_computation.7 | async-start | bytes 2293760 | tf_op jit(solution)/shard_map/reduce_scatter | solution.py:120
  13.8 1.8 copy-start.8
  15.6 4.5 %copy-start.6 = (s32[8]{0:T(128)S(1)}, s32[8]{0:T(128)}, u32[]{:S(2)}) copy-start(s32[8]{0:T(128)} %param.10) | copy-start | bytes 100
  19.3 48.4 %copy-start.4 = (bf16[128,1024]{1,0:T(8,128)(2,1)S(1)}, bf16[128,1024]{1,0:T(8,128)(2,1)}, u32[]{:S(2)}) copy-start(bf16[128,1024]{1,0:T(8,128)(2,1)} %param.15) | copy-start | bytes 786436
  19.3 48.5 %copy-start.5 = (bf16[128,1024]{1,0:T(8,128)(2,1)S(1)}, bf16[128,1024]{1,0:T(8,128)(2,1)}, u32[]{:S(2)}) copy-start(bf16[128,1024]{1,0:T(8,128)(2,1)} %param.8) | copy-start | bytes 786436
  21.0 43.0 %all-to-all-start.1 = ((s32[1,8,1,1]{3,2,0,1:T(1,128)}), s32[1,8,1,1]{3,2,0,1:T(1,128)S(1)}, u32[]{:S(2)}, u32[]{:S(2)}) async-start(s32[1,8,1,1]{3,2,0,1:T(1,128)} %copy.113), calls=%async_computation.2 | async-start | bytes 8192 | tf_op jit(solution)/shard_map/all_to_all | solution.py:139
  64.0 12.7 %all-to-all-start = ((bf16[32,8,1,896]{3,0,2,1:T(8,128)(2,1)}), bf16[32,8,1,896]{3,0,2,1:T(8,128)(2,1)S(1)}, u32[]{:S(2)}, u32[]{:S(2)}) async-start(bf16[32,8,1,896]{3,0,2,1:T(8,128)(2,1)} %copy.111), calls=%async_computation.1 | async-start | bytes 917504 | tf_op jit(solution)/shard_map/all_to_all | solution.py:132
  67.7 119.8 %all-reduce.3.cloned.1.call-start = ((), (), s32[]{:S(2)}) async-start(), calls=%async_computation.12 | async-start | bytes 1835008
  96.2 4.9 %copy-start.3 = (bf16[128,4,896]{2,1,0:T(4,128)(2,1)}, bf16[128,4,896]{2,1,0:T(4,128)(2,1)S(1)}, u32[]{:S(2)}) copy-start(bf16[128,4,896]{2,1,0:T(4,128)(2,1)S(1)} %all_gather.6) | copy-start | bytes 2752516
  101.8 2.3 copy-start.1
  102.8 1.3 copy-start.2
  134.7 6.8 %copy-start.7 = (u32[32]{0:T(128)S(1)}, u32[32]{0:T(128)}, u32[]{:S(2)}) copy-start(u32[32]{0:T(128)} %constant.68) | copy-start | bytes 388
  141.5 99.9 %all-gather.2.cloned.1.call-start = ((), (), s32[]{:S(2)}) async-start(), calls=%async_computation.9 | async-start | bytes 2293760 | tf_op jit(solution)/shard_map/all_gather | solution.py:189
  202.4 89.9 %reduce-scatter.7.cloned.1.call-start = ((), (), s32[]{:S(2)}) async-start(), calls=%async_computation.8 | async-start | bytes 4128768 | tf_op jit(solution)/shard_map/reduce_scatter | solution.py:175
  208.3 126.5 %reduce-scatter.9.cloned.1.call-start = ((), (), s32[]{:S(2)}) async-start(), calls=%async_computation.10 | async-start | bytes 1806336 | tf_op jit(solution)/shard_map/reduce_scatter | solution.py:199
  250.8 126.1 %reduce-scatter.11.cloned.1.call-start = ((), (), s32[]{:S(2)}) async-start(), calls=%async_computation.11 | async-start | bytes 1806336 | tf_op jit(solution)/shard_map/reduce_scatter | solution.py:202
Sparse Core Ops, SparseCore 0:
  19.4 42.1 reduce-scatter.4
  141.6 45.8 all-reduce.2
  202.5 38.8 all-gather.1
  244.7 47.6 reduce-scatter.6
  296.0 38.7 reduce-scatter.8
  338.1 38.7 reduce-scatter.10
where the time goes:
time: 386 us; the launch traced here: 385 us
  waiting for transfers between devices  224 us (58%)
  matrix products  71.2 us (18%)
  blocking collectives  31.7 us (8%)
  local copies, waits for them, and re-layouts  25.7 us (7%)
  between operations  15.7 us (4%)
  starting transfers between devices  9.3 us (2%)
  other arithmetic  7.31 us (2%)
    unnamed x7, waiting for transfers between devices  44.8 us
    reduce_scatter x1, waiting for transfers between devices, per_device(): lax.psum_scatter(out_total.astype(jnp.bfloat16), 'dp', scatter_dimension=...  40.4 us
    reduce_scatter x1, waiting for transfers between devices, per_device(): lax.psum_scatter(in_total.astype(jnp.bfloat16), 'dp', scatter_dimension=0...  40.1 us
    reduce_scatter x1, waiting for transfers between devices, per_device(): lax.psum_scatter(jnp.dot(picked, out_weight, preferred_element_type=jnp.f...  35.5 us
    all_gather x1, waiting for transfers between devices, per_device(): piece = lax.all_gather(slot_grads, 'mp', axis=0, tiled=True)  33 us
    reduce_scatter x1, waiting for transfers between devices, per_device(): lax.psum_scatter(kv_terms.astype(jnp.bfloat16), 'dp', scatter_dimension=0...  22.1 us
    all_gather x1, blocking collectives, per_device(): piece = lax.all_gather(slices, 'mp', axis=0, tiled=True)  19.2 us
    all_to_all x1, blocking collectives, per_device(): lax.all_to_all(returned, 'dp', split_axis=1, concat_axis=1, tiled=True)  12.5 us
  transfers between devices with their start and end apart: 8, of which 7 were waited for; matrix products, arithmetic and copies ran while one was open for 11% of the time, Pallas kernels for 0%

commit v1 on v0

v1 whole, which is shorter than its diff:
```python
import functools

import jax
import jax.numpy as jnp
from jax import lax
from jax.experimental import pallas as pl
from jax.experimental.pallas import tpu as pltpu
from jax.sharding import PartitionSpec as P

DH = 128
SPAN = 64
NEIGH = 2
TAG_ROWS = 16
VMEM_BYTES = 40 * 1024 * 1024


GELU_C = 0.7978845608028654
GELU_A = 0.044715
EPSILON = 1e-06

WHOLE = pl.BlockSpec(memory_space=pltpu.VMEM)


def gelu_value(values):
    inner = GELU_C * (values + GELU_A * values * values * values)
    return 0.5 * values * (1.0 + jnp.tanh(inner))


def gelu_slope(values):
    inner = GELU_C * (values + GELU_A * values * values * values)
    tanh_value = jnp.tanh(inner)
    return 0.5 * (1.0 + tanh_value) + 0.5 * values * (1.0 - tanh_value * tanh_value) * GELU_C * (
        1.0 + 3.0 * GELU_A * values * values
    )


def rms_normed(rows):
    wide = rows.astype(jnp.float32)
    mean_square = jnp.mean(wide * wide, axis=-1, keepdims=True)
    return (wide * lax.rsqrt(mean_square + EPSILON)).astype(jnp.bfloat16)


def ring_peer(axis, step):
    size = lax.axis_size(axis)
    return {axis: lax.rem(lax.axis_index(axis) + step, size)}


def flip_partner(bit):
    me = lax.axis_index("dp")
    mine = lax.rem(lax.div(me, 1 << bit), 2)
    return {"dp": me + (1 - 2 * mine) * (1 << bit)}, mine


def greet(peers):
    barrier = pltpu.get_barrier_semaphore()
    for peer in peers:
        pl.semaphore_signal(barrier, inc=1, device_id=peer, device_id_type=pl.DeviceIdType.MESH)
    pl.semaphore_wait(barrier, len(peers))


def remote(src, dst, send_sem, recv_sem, peer):
    return pltpu.make_async_remote_copy(
        src_ref=src,
        dst_ref=dst,
        send_sem=send_sem,
        recv_sem=recv_sem,
        device_id=peer,
        device_id_type=pl.DeviceIdType.MESH,
    )


class SumOverMp:
    def __init__(self, size, part, raw, out, landing, sems):
        self.size, self.part, self.raw, self.out, self.landing = size, part, raw, out, landing
        self.send1, self.recv1, self.send2, self.recv2 = sems
        self.me = lax.axis_index("mp")

    def scatter(self, step):
        peer = ring_peer("mp", step)
        return remote(
            self.part.at[peer["mp"]],
            self.landing.at[step - 1],
            self.send1.at[step - 1],
            self.recv1.at[step - 1],
            peer,
        )

    def gather(self, step):
        return remote(
            self.out.at[self.me],
            self.out.at[self.me],
            self.send2.at[step - 1],
            self.recv2.at[step - 1],
            ring_peer("mp", step),
        )

    def begin(self):
        for step in range(1, self.size):
            self.scatter(step).start()

    def reduce(self):
        total = self.part[self.me].astype(jnp.float32)
        for step in range(1, self.size):
            self.scatter(step).wait_recv()
            total = total + self.landing[step - 1].astype(jnp.float32)
        if self.raw is not None:
            total = total + self.raw[self.me].astype(jnp.float32)
        self.out[self.me] = total.astype(jnp.bfloat16)
        for step in range(1, self.size):
            self.gather(step).start()

    def finish(self):
        for step in range(1, self.size):
            self.gather(step).wait_recv()
        for step in range(1, self.size):
            self.scatter(step).wait_send()
            self.gather(step).wait_send()


class HalvingOverDp:
    def __init__(self, bits, source, out, buffers, sends, recvs):
        self.bits, self.source, self.out, self.buffers = bits, source, out, buffers
        self.sends, self.recvs = sends, recvs
        self.flips = [flip_partner(bit) for bit in bits]
        self.stages = len(bits)

    def held(self, stage, group, low):
        if stage > 0:
            return self.buffers[stage - 1].at[2 * group + low]
        rest = sum(((group >> s) & 1) << bit for s, bit in enumerate(self.bits[1:]))
        return self.source.at[rest + low * (1 << self.bits[0])]

    def held_dynamic(self, stage, group_base, group_low, low):
        if stage > 0:
            return self.buffers[stage - 1].at[2 * (2 * group_base + group_low) + low]
        rest = sum(((group_base >> s) & 1) << bit for s, bit in enumerate(self.bits[2:]))
        return self.source.at[rest + group_low * (1 << self.bits[1]) + low * (1 << self.bits[0])]

    def copy(self, stage, group, group_low):
        peer, mine = self.flips[stage]
        if stage == self.stages - 1:
            src, slot = self.held(stage, group, 1 - mine), group
        else:
            src = self.held_dynamic(stage, group, group_low, 1 - mine)
            slot = 2 * group + group_low
        return remote(
            src,
            self.buffers[stage].at[slot],
            self.sends[stage].at[slot],
            self.recvs[stage].at[slot],
            peer,
        )

    def orders(self, stage):
        if stage == self.stages - 1:
            return [(0, 0)]
        next_mine = self.flips[stage + 1][1]
        count = 1 << (self.stages - stage - 2)
        return [(g, 1 - next_mine) for g in range(count)] + [(g, next_mine) for g in range(count)]

    def begin(self):
        for group, low in self.orders(0):
            self.copy(0, group, low).start()

    def step(self, stage):
        mine = self.flips[stage][1]
        orders = self.orders(stage)
        ahead = self.orders(stage + 1)
        count = len(orders) // 2
        buffer = self.buffers[stage]
        for place, (group, low) in enumerate(orders):
            self.copy(stage, group, low).wait_recv()
            slot = 2 * group + low
            kept = self.held_dynamic(stage, group, low, mine)[...].astype(jnp.float32)
            buffer[slot] = (kept + buffer[slot].astype(jnp.float32)).astype(jnp.bfloat16)
            if place == count - 1:
                for next_group, next_low in ahead:
                    self.copy(stage + 1, next_group, next_low).start()

    def last(self):
        stage = self.stages - 1
        mine = self.flips[stage][1]
        self.copy(stage, 0, 0).wait_recv()
        kept = self.held(stage, 0, mine)[...].astype(jnp.float32)
        self.out[...] = kept + self.buffers[stage][0].astype(jnp.float32)

    def finish(self):
        for stage in range(self.stages):
            for group, low in self.orders(stage):
                self.copy(stage, group, low).wait_send()


def dp_bits(count):
    total = count.bit_length() - 1
    forward = list(range(total))
    return forward, forward[:1] + forward[:0:-1]


def halving_scratch(count, chunk):
    stages = count.bit_length() - 1
    sizes = [count >> (stage + 1) for stage in range(stages)]
    return (
        [pltpu.VMEM((size,) + chunk, jnp.bfloat16) for size in sizes]
        + [pltpu.SemaphoreType.DMA((size,)) for size in sizes]
        + [pltpu.SemaphoreType.DMA((size,)) for size in sizes]
    )


def halving_of(bits, source, out, scratch):
    stages = len(bits)
    return HalvingOverDp(
        bits, source, out, scratch[:stages], scratch[stages : 2 * stages], scratch[2 * stages :]
    )


def mp_scratch(size, rows, width):
    return [pltpu.VMEM((size - 1, rows, width), jnp.bfloat16)] + [
        pltpu.SemaphoreType.DMA((size - 1,)) for _ in range(4)
    ]


def params(collective_id):
    return pltpu.CompilerParams(
        collective_id=collective_id, has_side_effects=True, vmem_limit_bytes=VMEM_BYTES
    )


def mp_peers():
    return [ring_peer("mp", step) for step in range(1, lax.axis_size("mp"))]


def dp_flip_peers(count):
    return [flip_partner(bit)[0] for bit in range(count.bit_length() - 1)]


def route_kernel(n_dp, n_mp, message, out, landing, send1, recv1, send2, recv2):
    greet([ring_peer("dp", step) for step in range(1, n_dp)] + mp_peers())
    blocks = out.shape[0]
    rows = message.shape[1] - TAG_ROWS
    me_dp, me_mp = lax.axis_index("dp"), lax.axis_index("mp")

    def exchange(step):
        peer = ring_peer("dp", step)
        return remote(
            message.at[peer["dp"]],
            landing.at[step - 1],
            send1.at[step - 1],
            recv1.at[step - 1],
            peer,
        )

    for step in range(1, n_dp):
        exchange(step).start()
    data = message[me_dp, :rows].astype(jnp.float32)
    tag = message[me_dp, rows:].astype(jnp.float32)[:1]
    placed = [jnp.where(tag == block + 1.0, data, 0.0) for block in range(blocks)]
    for step in range(1, n_dp):
        exchange(step).wait_recv()
        data = landing[step - 1, :rows].astype(jnp.float32)
        tag = landing[step - 1, rows:].astype(jnp.float32)[:1]
        placed = [
            jnp.where(tag == block + 1.0, data, placed[block]) for block in range(blocks)
        ]
    mine = pl.ds(pl.multiple_of(me_mp * rows, rows), rows)
    for block in range(blocks):
        out[block, mine] = placed[block].astype(jnp.bfloat16)

    def gather(step):
        return remote(
            out.at[:, mine],
            out.at[:, mine],
            send2.at[step - 1],
            recv2.at[step - 1],
            ring_peer("mp", step),
        )

    for step in range(1, n_mp):
        gather(step).start()
    for step in range(1, n_mp):
        gather(step).wait_recv()
    for step in range(1, n_dp):
        exchange(step).wait_send()
    for step in range(1, n_mp):
        gather(step).wait_send()


def route(message, n_dp, n_mp, blocks, length):
    tall, width = message.shape[1:]
    return pl.pallas_call(
        functools.partial(route_kernel, n_dp, n_mp),
        out_shape=jax.ShapeDtypeStruct((blocks, length, width), jnp.bfloat16),
        in_specs=[WHOLE],
        out_specs=WHOLE,
        scratch_shapes=[
            pltpu.VMEM((n_dp - 1, tall, width), jnp.bfloat16),
            pltpu.SemaphoreType.DMA((n_dp - 1,)),
            pltpu.SemaphoreType.DMA((n_dp - 1,)),
            pltpu.SemaphoreType.DMA((n_mp - 1,)),
            pltpu.SemaphoreType.DMA((n_mp - 1,)),
        ],
        compiler_params=params(0),
        name="route",
    )(message)


def sum_kernel(n_mp, part, raw, out, landing, *sems):
    greet(mp_peers())
    total = SumOverMp(n_mp, part, raw, out, landing, sems)
    total.begin()
    total.reduce()
    total.finish()


def sum_over_mp(part, raw, n_mp):
    rows, width = part.shape[1:]
    return pl.pallas_call(
        functools.partial(sum_kernel, n_mp),
        out_shape=jax.ShapeDtypeStruct(part.shape, jnp.bfloat16),
        in_specs=[WHOLE, WHOLE],
        out_specs=WHOLE,
        scratch_shapes=mp_scratch(n_mp, rows, width),
        compiler_params=params(1),
        name="sum_encoded",
    )(part, raw)


def back_kernel(n_mp, n_dp, part, first, second, out, out_first, out_second, landing, *rest):
    greet(mp_peers() + dp_flip_peers(n_dp))
    sems, rest = rest[:4], rest[4:]
    half = len(rest) // 2
    bits = dp_bits(n_dp)
    total = SumOverMp(n_mp, part, None, out, landing, sems)
    pair = [
        halving_of(bits[0], first, out_first, rest[:half]),
        halving_of(bits[1], second, out_second, rest[half:]),
    ]
    total.begin()
    for one in pair:
        one.begin()
    for one in pair:
        one.step(0)
    total.reduce()
    for stage in range(1, len(bits[0]) - 1):
        for one in pair:
            one.step(stage)
    for one in pair:
        one.last()
    total.finish()
    for one in pair:
        one.finish()


def back_sums(part, first, second, n_mp, n_dp):
    rows, width = part.shape[1:]
    chunk = first.shape[1:]
    return pl.pallas_call(
        functools.partial(back_kernel, n_mp, n_dp),
        out_shape=(
            jax.ShapeDtypeStruct(part.shape, jnp.bfloat16),
            jax.ShapeDtypeStruct(chunk, jnp.float32),
            jax.ShapeDtypeStruct(chunk, jnp.float32),
        ),
        in_specs=[WHOLE] * 3,
        out_specs=(WHOLE,) * 3,
        scratch_shapes=mp_scratch(n_mp, rows, width)
        + halving_scratch(n_dp, chunk)
        + halving_scratch(n_dp, chunk),
        compiler_params=params(2),
        name="sum_back",
    )(part, first, second)


def grads_kernel(n_dp, first, second, out_first, out_second, *rest):
    greet(dp_flip_peers(n_dp))
    half = len(rest) // 2
    bits = dp_bits(n_dp)
    pair = [
        halving_of(bits[0], first, out_first, rest[:half]),
        halving_of(bits[1], second, out_second, rest[half:]),
    ]
    for one in pair:
        one.begin()
    for stage in range(len(bits[0]) - 1):
        for one in pair:
            one.step(stage)
    for one in pair:
        one.last()
    for one in pair:
        one.finish()


def grad_sums(first, second, n_dp):
    chunk = first.shape[1:]
    return pl.pallas_call(
        functools.partial(grads_kernel, n_dp),
        out_shape=(
            jax.ShapeDtypeStruct(chunk, jnp.float32),
            jax.ShapeDtypeStruct(chunk, jnp.float32),
        ),
        in_specs=[WHOLE] * 2,
        out_specs=(WHOLE,) * 2,
        scratch_shapes=halving_scratch(n_dp, chunk) + halving_scratch(n_dp, chunk),
        compiler_params=params(3),
        name="sum_grads",
    )(first, second)


def matmul(left, right, left_dim, right_dim):
    return lax.dot_general(
        left, right, (((left_dim,), (right_dim,)), ((), ())), preferred_element_type=jnp.float32
    )


def attend_kernel(spans, queries, keys, values, grads, context, d_queries, d_keys, d_values):
    scaling = DH ** (-0.5)
    wide = keys.shape[0] // spans
    for span in range(spans):
        own = pl.ds(span * SPAN, SPAN)
        seen = pl.ds(span * wide, wide)
        q, g = queries[own, :], grads[own, :]
        k, v = keys[seen, :], values[seen, :]
        scores = matmul(q, k, 1, 1) * scaling
        weights = jnp.exp(scores - jnp.max(scores, axis=-1, keepdims=True))
        probs_wide = weights / jnp.sum(weights, axis=-1, keepdims=True)
        probs = probs_wide.astype(jnp.bfloat16)
        context[own, :] = matmul(probs, v, 1, 0).astype(jnp.bfloat16)
        d_probs = matmul(g, v, 1, 1)
        inner = jnp.sum(d_probs * probs_wide, axis=-1, keepdims=True)
        d_scores = (probs_wide * (d_probs - inner) * scaling).astype(jnp.bfloat16)
        d_queries[own, :] = matmul(d_scores, k, 1, 0).astype(jnp.bfloat16)
        d_keys[seen, :] = matmul(d_scores, q, 0, 0).astype(jnp.bfloat16)
        d_values[seen, :] = matmul(probs, g, 0, 0).astype(jnp.bfloat16)


def attend(queries, keys, values, grads, spans):
    rows, columns = queries.shape
    count = keys.shape[0]
    narrow = pl.BlockSpec((rows, DH), lambda head: (0, head))
    tall = pl.BlockSpec((count, DH), lambda head: (0, head))
    small = jax.ShapeDtypeStruct((rows, columns), jnp.bfloat16)
    large = jax.ShapeDtypeStruct((count, columns), jnp.bfloat16)
    return pl.pallas_call(
        functools.partial(attend_kernel, spans),
        out_shape=(small, small, large, large),
        grid=(columns // DH,),
        in_specs=[narrow, tall, tall, narrow],
        out_specs=(narrow, narrow, tall, tall),
        compiler_params=pltpu.CompilerParams(vmem_limit_bytes=VMEM_BYTES),
        name="attend",
    )(queries, keys, values, grads)


def per_device(queries, neighbours, targets, counts, in_weight, out_weight, kv_weight, d_context):
    length, holding, width = neighbours.shape
    n_dp, n_mp = lax.axis_size("dp"), lax.axis_size("mp")
    slice_rows = length // n_mp
    spans = queries.shape[0] // SPAN
    blocks = NEIGH * spans
    tokens = blocks * length
    is_live = jnp.arange(holding, dtype=jnp.int32) < counts[0]
    owners = jnp.arange(n_dp, dtype=jnp.int32)
    chosen = jnp.logical_and((targets // blocks)[None, :] == owners[:, None], is_live[None, :])
    tags = jnp.sum(jnp.where(chosen, (targets % blocks)[None, :] + 1, 0), axis=1)
    own = lax.dynamic_slice_in_dim(neighbours, lax.axis_index("mp") * slice_rows, slice_rows, 0)
    moved = jnp.einsum(
        "oh,thd->otd", chosen.astype(jnp.bfloat16), own, preferred_element_type=jnp.float32
    ).astype(jnp.bfloat16)
    tag_rows = jnp.broadcast_to(
        tags.astype(jnp.bfloat16)[:, None, None], (n_dp, TAG_ROWS, width)
    )
    message = jnp.concatenate([moved, tag_rows], axis=1)
    raw = route(message, n_dp, n_mp, blocks, length).reshape(tokens, width)

    normed = rms_normed(raw)
    hidden_pre = jnp.dot(normed, in_weight, preferred_element_type=jnp.float32)
    activated = gelu_value(hidden_pre).astype(jnp.bfloat16)
    part = jnp.dot(activated, out_weight, preferred_element_type=jnp.float32).astype(jnp.bfloat16)
    sliced = (n_mp, tokens // n_mp, width)
    encoded = sum_over_mp(part.reshape(sliced), raw.reshape(sliced), n_mp).reshape(tokens, width)

    key_weight, value_weight = kv_weight[:, 0], kv_weight[:, 1]
    keys = jnp.dot(encoded, key_weight, preferred_element_type=jnp.float32).astype(jnp.bfloat16)
    values = jnp.dot(encoded, value_weight, preferred_element_type=jnp.float32).astype(
        jnp.bfloat16
    )
    context, d_queries, d_keys, d_values = attend(queries, keys, values, d_context, spans)

    back = (matmul(d_keys, key_weight, 1, 1) + matmul(d_values, value_weight, 1, 1)).astype(
        jnp.bfloat16
    )
    chunked = (n_dp, width // n_dp, -1)
    key_terms = matmul(encoded, d_keys, 0, 0).astype(jnp.bfloat16).reshape(chunked)
    value_terms = matmul(encoded, d_values, 0, 0).astype(jnp.bfloat16).reshape(chunked)
    d_encoded, grad_key, grad_value = back_sums(
        back.reshape(sliced), key_terms, value_terms, n_mp, n_dp
    )
    d_encoded = d_encoded.reshape(tokens, width)

    d_act = matmul(d_encoded, out_weight, 1, 1)
    d_pre = (d_act * gelu_slope(hidden_pre)).astype(jnp.bfloat16)
    in_terms = matmul(normed, d_pre, 0, 0).astype(jnp.bfloat16).reshape(chunked)
    out_terms = matmul(d_encoded, activated, 0, 0).astype(jnp.bfloat16).reshape(chunked)
    grad_in, grad_out_t = grad_sums(in_terms, out_terms, n_dp)
    return (
        context,
        d_queries,
        jnp.stack([grad_key, grad_value], axis=1),
        grad_in,
        grad_out_t.T,
    )


def solution(mesh):
    placed = (
        P("dp", "mp"),
        P(None, "dp", None),
        P("dp"),
        P("dp"),
        P(None, "mp"),
        P("mp", None),
        P(None, None, "mp"),
        P("dp", "mp"),
    )
    return jax.shard_map(
        per_device,
        mesh=mesh,
        in_specs=placed,
        out_specs=(P("dp", "mp"), P("dp", "mp"), P("dp", None, "mp"), P("dp", "mp"), P("mp", "dp")),
        check_vma=False,
    )
```

time: 386 us -> 184 us (0.48)
  waiting for transfers between devices: 224 us -> 0 us
  Pallas kernels: 0 us -> 151 us
  matrix products: 71.2 us -> 18.5 us
  blocking collectives: 31.7 us -> 0 us
  local copies, waits for them, and re-layouts: 25.7 us -> 10.5 us
  between operations: 15.7 us -> 1.67 us
  starting transfers between devices: 9.3 us -> 0 us
  other arithmetic: 7.31 us -> 1.43 us
    pallas_call x0 -> x5, Pallas kernels: none -> 151 us  [the longest x1 45.5 us: back_sums(): pl.pallas_call(functools.partial(back_kernel, n_mp, n_dp), out_shape=(jax...]
    reduce_scatter x4 -> x0, waiting for transfers between devices: 138 us -> none  [the longest x1 40.4 us: per_device(): lax.psum_scatter(out_total.astype(jnp.bfloat16), 'dp', scatter_dimension=...]
    dot_general x17 -> x11, matrix products: 71.2 us -> 18.5 us  [the longest x6 13.1 us: matmul(): lax.dot_general(left, right, (((left_dim,), (right_dim,)), ((), ())), pre...]
    unnamed x7 -> x0, waiting for transfers between devices: 44.8 us -> none
    all_gather x1 -> x0, waiting for transfers between devices: 33 us -> none  [per_device(): piece = lax.all_gather(slot_grads, 'mp', axis=0, tiled=True)]
    all_gather x1 -> x0, blocking collectives: 19.2 us -> none  [per_device(): piece = lax.all_gather(slices, 'mp', axis=0, tiled=True)]
    all_to_all x1 -> x0, blocking collectives: 12.5 us -> none  [per_device(): lax.all_to_all(returned, 'dp', split_axis=1, concat_axis=1, tiled=True)]
    all_to_all x2 -> x0, starting transfers between devices: 8.8 us -> none  [the longest x1 5.17 us: per_device(): lax.all_to_all(sent_place, 'dp', split_axis=1, concat_axis=1, tiled=True)]
  transfers between devices with their start and end apart: 8 -> 0, of which waited for: 7 -> 0; matrix products, arithmetic and copies ran while one was open for 11% -> 0% of each run, Pallas kernels for 0% -> 0%
where the time goes in v1:
time: 184 us; the launch traced here: 183 us
  Pallas kernels  151 us (82%)
  matrix products  18.5 us (10%)
  local copies, waits for them, and re-layouts  10.5 us (6%)
    pallas_call x1, Pallas kernels, back_sums(): pl.pallas_call(functools.partial(back_kernel, n_mp, n_dp), out_shape=(jax...  45.5 us
    pallas_call x1, Pallas kernels, sum_over_mp(): pl.pallas_call(functools.partial(sum_kernel, n_mp), out_shape=jax.ShapeDt...  43.3 us
    pallas_call x1, Pallas kernels, route(): pl.pallas_call(functools.partial(route_kernel, n_dp, n_mp), out_shape=jax...  30.6 us
    pallas_call x1, Pallas kernels, grad_sums(): pl.pallas_call(functools.partial(grads_kernel, n_dp), out_shape=(jax.Shap...  19.7 us
    dot_general x6, matrix products, matmul(): lax.dot_general(left, right, (((left_dim,), (right_dim,)), ((), ())), pre...  13.1 us
    pallas_call x1, Pallas kernels, attend(): pl.pallas_call(functools.partial(attend_kernel, spans), out_shape=(small,...  11.6 us
    slice x1, local copies, waits for them, and re-layouts, per_device(): key_weight, value_weight = (kv_weight[:, 0], kv_weight[:, 1])  5.22 us
    unnamed x21, local copies, waits for them, and re-layouts  5.17 us

profile of v1, /device:TPU:0, one launch (start us, length us, event | category | flops | bytes accessed | tf_op | source)
XLA Modules:
  0.0 182.8 jit_solution(694433476220613027)
XLA Ops:
  0.6 0.0 copy-start
  1.4 0.7 and_select_fusion.1
  2.1 0.1 select_reduce_fusion
  2.2 0.1 broadcast_in_dim.16
  2.3 0.3 fusion.14
  2.6 0.1 copy.28
  2.7 0.1 pad_maximum_fusion.1.message
  2.8 30.6 %route.1.raw = bf16[4,128,896]{2,1,0:T(8,128)(2,1)S(1)} custom-call(bf16[8,48,896]{2,1,0:T(8,128)(2,1)S(1)} %pad_maximum_fusion.1.message), custom_call_target="tpu_custom_call" | custom-call | tf_op jit(solution)/shard_map/route/pallas_call | solution.py:289
  33.3 0.3 multiply_reduce_fusion
  33.6 0.2 fusion.7
  33.8 1.0 copy-done.5
  34.8 1.2 fusion.29
  36.0 0.2 copy-done.7
  36.2 1.3 convolution_convert_fusion.6
  37.5 43.3 %sum_encoded.1 = bf16[4,128,896]{2,1,0:T(8,128)(2,1)S(1)} custom-call(bf16[4,128,896]{2,1,0:T(8,128)(2,1)S(1)} %bitcast.54, bf16[4,128,896]{2,1,0:T(8,128)(2,1)S(1)} %route.1.raw), custom_call_target="tpu_custom_call" | custom-call | tf_op jit(solution)/shard_map/sum_encoded/pallas_call | solution.py:316
  80.8 5.2 %fusion.28 = (bf16[896,1,1024]{2,1,0:T(2,128)(2,1)S(1)}, bf16[896,1,1024]{2,1,0:T(2,128)(2,1)S(1)}) fusion(bf16[896,2,1024]{2,1,0:T(2,128)(2,1)S(1)} %copy-done.4), kind=kLoop, calls=%fused_computation.54 | loop fusion | bytes 7340032 | tf_op jit(solution)/shard_map/slice | solution.py:481
  86.1 1.3 convolution_convert_fusion.4.values
  87.4 1.3 convolution_convert_fusion.5.keys
  88.7 11.6 %attend.1 = (bf16[128,1024]{1,0:T(8,128)(2,1)}, bf16[128,1024]{1,0:T(8,128)(2,1)}, bf16[512,1024]{1,0:T(8,128)(2,1)S(1)}, bf16[512,1024]{1,0:T(8,128)(2,1)S(1)}) custom-call(bf16[128,1024]{1,0:T(8,128)(2,1)S(1)} %copy-done.1, bf16[512,1024]{1,0:T(8,128)(2,1)S(1)} %convolution_convert_fusion.5.keys, bf16[512,1024]{1,0:T(8,128)(2,1)S(1)} %convolution_convert_fusion.4.values, ...), custom_call_target="tpu_custom_call" | custom-call | tf_op jit(solution)/shard_map/attend/pallas_call | solution.py:442
  100.4 1.3 fusion.13
  101.7 1.4 add_convert_fusion
  103.1 1.1 convolution_convert_fusion.1
  104.2 1.1 convolution_convert_fusion
  105.4 45.5 %sum_back.1 = (bf16[4,128,896]{2,1,0:T(8,128)(2,1)S(1)}, f32[112,1024]{1,0:T(8,128)S(1)}, f32[112,1024]{1,0:T(8,128)S(1)}) custom-call(bf16[4,128,896]{2,1,0:T(8,128)(2,1)S(1)} %bitcast.53, bf16[8,112,1024]{2,1,0:T(8,128)(2,1)S(1)} %bitcast.45, bf16[8,112,1024]{2,1,0:T(8,128)(2,1)S(1)} %bitcast.46), custom_call_target="tpu_custom_call" | custom-call | tf_op jit(solution)/shard_map/sum_back/pallas_call | solution.py:356
  150.9 0.1 pad_maximum_fusion
  151.0 0.8 copy-done.3
  151.8 1.6 copy.18
  153.4 5.1 %convolution_convert_fusion.3 = bf16[896,896]{1,0:T(8,128)(2,1)S(1)} fusion(bf16[512,896]{1,0:T(8,128)(2,1)} %copy-done.5, f32[512,896]{1,0:T(8,128)} %copy-done.8, bf16[512,896]{1,0:T(8,128)(2,1)} %bitcast.58, bf16[896,896]{1,0:T(8,128)(2,1)} %param.13), kind=kOutput, calls=%fused_computation.19 | convolution fusion | flops 1653686272 | bytes 6881280 | tf_op jit(solution)/shard_map/dot_general | solution.py:409
  158.5 3.1 %convolution_convert_fusion.2 = bf16[896,896]{1,0:T(8,128)(2,1)S(1)} fusion(bf16[512,896]{1,0:T(8,128)(2,1)} %bitcast.59, f32[512,896]{1,0:T(8,128)} %copy-done.8), kind=kOutput, calls=%fused_computation.18 | convolution fusion | flops 827015168 | bytes 4358144 | tf_op jit(solution)/shard_map/dot_general | solution.py:409
  161.6 19.7 %sum_grads.1 = (f32[112,896]{1,0:T(8,128)S(1)}, f32[112,896]{1,0:T(8,128)S(1)}) custom-call(bf16[8,112,896]{2,1,0:T(8,128)(2,1)S(1)} %bitcast.47, bf16[8,112,896]{2,1,0:T(8,128)(2,1)S(1)} %bitcast.48), custom_call_target="tpu_custom_call" | custom-call | tf_op jit(solution)/shard_map/sum_grads/pallas_call | solution.py:394
  181.3 0.8 copy.32
  182.0 0.7 copy.33
  (17 shorter events, 0.1 us)
Async XLA Ops:
  0.6 1.7 copy-start
  2.7 32.0 %copy-start.6 = (bf16[896,896]{1,0:T(8,128)(2,1)S(1)}, bf16[896,896]{1,0:T(8,128)(2,1)}, u32[]{:S(2)}) copy-start(bf16[896,896]{1,0:T(8,128)(2,1)} %param.12) | copy-start | bytes 4816900
  33.8 1.0 copy-start.5
  34.8 1.4 copy-start.7
  36.2 1.3 copy-start.8
  36.2 44.6 %copy-start.4 = (bf16[896,2,1024]{2,1,0:T(2,128)(2,1)S(1)}, bf16[896,2,1024]{2,1,0:T(2,128)(2,1)}, u32[]{:S(2)}) copy-start(bf16[896,2,1024]{2,1,0:T(2,128)(2,1)} %param.14) | copy-start | bytes 11010052
  87.4 1.3 copy-start.1
  87.4 1.3 copy-start.2
  150.9 0.9 copy-start.3

commit v2 on v1

v2 whole, which is shorter than its diff:
```python
import functools

import jax
import jax.numpy as jnp
from jax import lax
from jax.experimental import pallas as pl
from jax.experimental.pallas import tpu as pltpu
from jax.sharding import PartitionSpec as P

DH = 128
SPAN = 64
NEIGH = 2
TAG_ROWS = 16
CHAIN_CHUNKS = 16
CHAIN_LAG = 2
CHAIN_WINDOW = 4
HEADS_AT_ONCE = 2
VMEM_BYTES = 40 * 1024 * 1024


GELU_C = 0.7978845608028654
GELU_A = 0.044715
EPSILON = 1e-06

WHOLE = pl.BlockSpec(memory_space=pltpu.VMEM)


def gelu_value(values):
    inner = GELU_C * (values + GELU_A * values * values * values)
    return 0.5 * values * (1.0 + jnp.tanh(inner))


def gelu_slope(values):
    inner = GELU_C * (values + GELU_A * values * values * values)
    tanh_value = jnp.tanh(inner)
    return 0.5 * (1.0 + tanh_value) + 0.5 * values * (1.0 - tanh_value * tanh_value) * GELU_C * (
        1.0 + 3.0 * GELU_A * values * values
    )


def rms_normed(rows):
    wide = rows.astype(jnp.float32)
    mean_square = jnp.mean(wide * wide, axis=-1, keepdims=True)
    return (wide * lax.rsqrt(mean_square + EPSILON)).astype(jnp.bfloat16)


def ring_peer(axis, step):
    size = lax.axis_size(axis)
    return {axis: lax.rem(lax.axis_index(axis) + step, size)}


def flip_partner(bit):
    me = lax.axis_index("dp")
    mine = lax.rem(lax.div(me, 1 << bit), 2)
    return {"dp": me + (1 - 2 * mine) * (1 << bit)}, mine


def greet(peers):
    barrier = pltpu.get_barrier_semaphore()
    for peer in peers:
        pl.semaphore_signal(barrier, inc=1, device_id=peer, device_id_type=pl.DeviceIdType.MESH)
    pl.semaphore_wait(barrier, len(peers))


def remote(src, dst, send_sem, recv_sem, peer):
    return pltpu.make_async_remote_copy(
        src_ref=src,
        dst_ref=dst,
        send_sem=send_sem,
        recv_sem=recv_sem,
        device_id=peer,
        device_id_type=pl.DeviceIdType.MESH,
    )


class ChainOverMp:
    def __init__(self, size, part, raw, out, scratch):
        self.size, self.part, self.raw, self.out = size, part, raw, out
        self.staged, self.landing, self.up_send, self.up_recv, self.out_send, self.out_recv = scratch
        self.me = lax.axis_index("mp")
        self.chunks = part.shape[0]
        self.is_end = jnp.logical_or(self.me == 0, self.me == size - 1)
        self.steps = self.chunks + CHAIN_LAG

    def root(self, chunk):
        return self.size // 2 - 1 + chunk % 2

    def up(self, chunk, toward, source):
        side = 0 if toward > 0 else 1
        return remote(
            source.at[chunk],
            self.landing.at[side, chunk],
            self.up_send.at[chunk],
            self.up_recv.at[side, chunk],
            {"mp": self.me + toward},
        )

    def outward(self, chunk, toward):
        side = 0 if toward > 0 else 1
        return remote(
            self.out.at[chunk],
            self.out.at[chunk],
            self.out_send.at[side, chunk],
            self.out_recv.at[chunk],
            {"mp": self.me + toward},
        )

    def arrived(self, chunk, toward):
        self.up(chunk, toward, self.staged).wait_recv()
        return self.landing[0 if toward > 0 else 1, chunk].astype(jnp.float32)

    def inner_up(self, chunk):
        root = self.root(chunk)
        own = self.part[chunk].astype(jnp.float32)
        for toward, here in ((1, self.me < root), (-1, self.me > root)):

            @pl.when(here)
            def _(toward=toward):
                total = own + self.arrived(chunk, toward)
                self.staged[chunk] = total.astype(jnp.bfloat16)
                self.up(chunk, toward, self.staged).start()

        @pl.when(self.me == root)
        def _():
            total = own + self.arrived(chunk, 1) + self.arrived(chunk, -1)
            if self.raw is not None:
                total = total + self.raw[chunk].astype(jnp.float32)
            self.out[chunk] = total.astype(jnp.bfloat16)
            self.outward(chunk, 1).start()
            self.outward(chunk, -1).start()

    def inner_down(self, chunk):
        root = self.root(chunk)
        for toward, here in ((-1, self.me < root), (1, self.me > root)):

            @pl.when(here)
            def _(toward=toward):
                self.outward(chunk, toward).wait_recv()
                self.outward(chunk, toward).start()

    def end_up(self, chunk):
        for toward, here in ((1, self.me == 0), (-1, self.me == self.size - 1)):

            @pl.when(here)
            def _(toward=toward):
                if chunk >= CHAIN_WINDOW:
                    self.up(chunk - CHAIN_WINDOW, toward, self.part).wait_send()
                self.up(chunk, toward, self.part).start()

    def step(self, index):
        @pl.when(self.is_end)
        def _():
            if index < self.chunks:
                self.end_up(index)

        @pl.when(jnp.logical_not(self.is_end))
        def _():
            if index < self.chunks:
                self.inner_up(index)
            if index >= CHAIN_LAG:
                self.inner_down(index - CHAIN_LAG)

    def finish(self):
        for toward, here in ((1, self.me == 0), (-1, self.me == self.size - 1)):

            @pl.when(here)
            def _(toward=toward):
                for chunk in range(self.chunks):
                    self.outward(chunk, toward).wait_recv()
                for chunk in range(self.chunks - CHAIN_WINDOW, self.chunks):
                    self.up(chunk, toward, self.part).wait_send()

        @pl.when(jnp.logical_not(self.is_end))
        def _():
            for chunk in range(self.chunks):
                root = self.root(chunk)
                for toward, here in ((1, self.me < root), (-1, self.me > root)):

                    @pl.when(here)
                    def _(toward=toward):
                        self.up(chunk, toward, self.staged).wait_send()
                        self.outward(chunk, -toward).wait_send()

                @pl.when(self.me == root)
                def _():
                    self.outward(chunk, 1).wait_send()
                    self.outward(chunk, -1).wait_send()


class HalvingOverDp:
    def __init__(self, bits, source, out, buffers, sends, recvs):
        self.bits, self.source, self.out, self.buffers = bits, source, out, buffers
        self.sends, self.recvs = sends, recvs
        self.flips = [flip_partner(bit) for bit in bits]
        self.stages = len(bits)

    def held(self, stage, group, low):
        wanted = (low,) + group
        if stage > 0:
            return self.buffers[stage - 1].at[self.slot(wanted)]
        return self.source.at[sum(value * (1 << bit) for value, bit in zip(wanted, self.bits))]

    def slot(self, group):
        return sum((value * (1 << place) for place, value in enumerate(group)), 0)

    def copy(self, stage, group):
        peer, mine = self.flips[stage]
        slot = self.slot(group)
        return remote(
            self.held(stage, group, 1 - mine),
            self.buffers[stage].at[slot],
            self.sends[stage].at[slot],
            self.recvs[stage].at[slot],
            peer,
        )

    def orders(self, stage):
        if stage == self.stages - 1:
            return [()]
        later = self.orders(stage + 1)
        mine = self.flips[stage + 1][1]
        return [(1 - mine,) + group for group in later] + [(mine,) + group for group in later]

    def begin(self):
        for group in self.orders(0):
            self.copy(0, group).start()

    def units(self):
        return [
            functools.partial(self.unit, stage, place)
            for stage in range(self.stages - 1)
            for place in range(len(self.orders(stage)))
        ] + [self.last]

    def unit(self, stage, place):
        mine = self.flips[stage][1]
        orders = self.orders(stage)
        group = orders[place]
        buffer = self.buffers[stage]
        self.copy(stage, group).wait_recv()
        slot = self.slot(group)
        kept = self.held(stage, group, mine)[...].astype(jnp.float32)
        buffer[slot] = (kept + buffer[slot].astype(jnp.float32)).astype(jnp.bfloat16)
        if place < len(orders) // 2:
            self.copy(stage + 1, self.orders(stage + 1)[place]).start()

    def last(self):
        stage = self.stages - 1
        mine = self.flips[stage][1]
        self.copy(stage, ()).wait_recv()
        kept = self.held(stage, (), mine)[...].astype(jnp.float32)
        self.out[...] = kept + self.buffers[stage][0].astype(jnp.float32)

    def finish(self):
        for stage in range(self.stages):
            for group in self.orders(stage):
                self.copy(stage, group).wait_send()


def dp_bits(count):
    total = count.bit_length() - 1
    forward = list(range(total))
    return forward, forward[:1] + forward[:0:-1]


def halving_scratch(count, chunk):
    stages = count.bit_length() - 1
    sizes = [count >> (stage + 1) for stage in range(stages)]
    return (
        [pltpu.VMEM((size,) + chunk, jnp.bfloat16) for size in sizes]
        + [pltpu.SemaphoreType.DMA((size,)) for size in sizes]
        + [pltpu.SemaphoreType.DMA((size,)) for size in sizes]
    )


def halving_of(bits, source, out, scratch):
    stages = len(bits)
    return HalvingOverDp(
        bits, source, out, scratch[:stages], scratch[stages : 2 * stages], scratch[2 * stages :]
    )


def mp_scratch(chunks, rows, width):
    return [
        pltpu.VMEM((chunks, rows, width), jnp.bfloat16),
        pltpu.VMEM((2, chunks, rows, width), jnp.bfloat16),
        pltpu.SemaphoreType.DMA((chunks,)),
        pltpu.SemaphoreType.DMA((2, chunks)),
        pltpu.SemaphoreType.DMA((2, chunks)),
        pltpu.SemaphoreType.DMA((chunks,)),
    ]


def params(collective_id):
    return pltpu.CompilerParams(
        collective_id=collective_id, has_side_effects=True, vmem_limit_bytes=VMEM_BYTES
    )


def mp_peers():
    return [ring_peer("mp", step) for step in range(1, lax.axis_size("mp"))]


def dp_flip_peers(count):
    return [flip_partner(bit)[0] for bit in range(count.bit_length() - 1)]


def route_kernel(n_dp, n_mp, straight, split, *refs):
    if straight:
        message, whole, out, landing, whole_landing, *sems = refs
    else:
        message, out, landing, *sems = refs
    greet([ring_peer("dp", step) for step in range(1, n_dp)] + mp_peers())
    blocks = out.shape[0]
    me_dp, me_mp = lax.axis_index("dp"), lax.axis_index("mp")

    def exchange(source, target, step, send, recv):
        peer = ring_peer("dp", step)
        return remote(
            source.at[peer["dp"]], target.at[step - 1], send.at[step - 1], recv.at[step - 1], peer
        )

    def parts(step):
        return exchange(message, landing, step, sems[0], sems[1])

    def wholes(step):
        return exchange(whole, whole_landing, step, sems[4], sems[5])

    others = range(1, n_dp)
    for step in others:
        parts(step).start()
    if straight:
        for step in others:
            wholes(step).start()

    def tags_of(rows):
        return rows.astype(jnp.float32)[:1]

    for step in others:
        parts(step).wait_recv()
    data_rows = pl.ds(0, split)
    tag_rows = pl.ds(split, TAG_ROWS)
    tags = [tags_of(message[me_dp, tag_rows])] + [
        tags_of(landing[step - 1, tag_rows]) for step in others
    ]

    def place(own, arrived, first, where):
        sources = [own[me_dp, first]] + [arrived[step - 1, first] for step in others]
        sources = [rows.astype(jnp.float32) for rows in sources]
        for block in range(blocks):
            value = jnp.zeros_like(sources[0])
            for tag, rows in zip(tags, sources):
                value = jnp.where(tag == block + 1.0, rows, value)
            out[block, where] = value.astype(jnp.bfloat16)

    mine = pl.ds(pl.multiple_of(straight + me_mp * split, 16), split)
    place(message, landing, data_rows, mine)

    def gather(step):
        return remote(
            out.at[:, mine],
            out.at[:, mine],
            sems[2].at[step - 1],
            sems[3].at[step - 1],
            ring_peer("mp", step),
        )

    for step in range(1, n_mp):
        gather(step).start()
    if straight:
        for step in others:
            wholes(step).wait_recv()
        for first in range(0, straight, 16):
            rows = pl.ds(first, 16)
            place(whole, whole_landing, rows, rows)
    for step in range(1, n_mp):
        gather(step).wait_recv()
    for step in others:
        parts(step).wait_send()
        if straight:
            wholes(step).wait_send()
    for step in range(1, n_mp):
        gather(step).wait_send()


def route(messages, n_dp, n_mp, blocks, length, straight, split):
    width = messages[0].shape[2]
    return pl.pallas_call(
        functools.partial(route_kernel, n_dp, n_mp, straight, split),
        out_shape=jax.ShapeDtypeStruct((blocks, length, width), jnp.bfloat16),
        in_specs=[WHOLE] * len(messages),
        out_specs=WHOLE,
        scratch_shapes=[
            pltpu.VMEM((n_dp - 1,) + message.shape[1:], jnp.bfloat16) for message in messages
        ]
        + [
            pltpu.SemaphoreType.DMA((n_dp - 1,)),
            pltpu.SemaphoreType.DMA((n_dp - 1,)),
            pltpu.SemaphoreType.DMA((n_mp - 1,)),
            pltpu.SemaphoreType.DMA((n_mp - 1,)),
            pltpu.SemaphoreType.DMA((n_dp - 1,)),
            pltpu.SemaphoreType.DMA((n_dp - 1,)),
        ],
        compiler_params=params(0),
        name="route",
    )(*messages)


def sum_kernel(n_mp, part, raw, out, *scratch):
    greet(mp_peers())
    total = ChainOverMp(n_mp, part, raw, out, scratch)
    for index in range(total.steps):
        total.step(index)
    total.finish()


def sum_over_mp(part, raw, n_mp):
    rows, width = part.shape[1:]
    return pl.pallas_call(
        functools.partial(sum_kernel, n_mp),
        out_shape=jax.ShapeDtypeStruct(part.shape, jnp.bfloat16),
        in_specs=[WHOLE, WHOLE],
        out_specs=WHOLE,
        scratch_shapes=mp_scratch(part.shape[0], rows, width),
        compiler_params=params(1),
        name="sum_encoded",
    )(part, raw)


def interleaved(pair):
    return [unit for both in zip(*(one.units() for one in pair)) for unit in both]


def back_kernel(n_mp, n_dp, part, first, second, out, out_first, out_second, *rest):
    greet(mp_peers() + dp_flip_peers(n_dp))
    chain, rest = rest[:6], rest[6:]
    half = len(rest) // 2
    bits = dp_bits(n_dp)
    total = ChainOverMp(n_mp, part, None, out, chain)
    pair = [
        halving_of(bits[0], first, out_first, rest[:half]),
        halving_of(bits[1], second, out_second, rest[half:]),
    ]
    for one in pair:
        one.begin()
    units = interleaved(pair)
    for index in range(total.steps):
        total.step(index)
        if index > 0 and units:
            units.pop(0)()
    for unit in units:
        unit()
    total.finish()
    for one in pair:
        one.finish()


def back_sums(part, first, second, n_mp, n_dp):
    rows, width = part.shape[1:]
    chunk = first.shape[1:]
    return pl.pallas_call(
        functools.partial(back_kernel, n_mp, n_dp),
        out_shape=(
            jax.ShapeDtypeStruct(part.shape, jnp.bfloat16),
            jax.ShapeDtypeStruct(chunk, jnp.float32),
            jax.ShapeDtypeStruct(chunk, jnp.float32),
        ),
        in_specs=[WHOLE] * 3,
        out_specs=(WHOLE,) * 3,
        scratch_shapes=mp_scratch(part.shape[0], rows, width)
        + halving_scratch(n_dp, chunk)
        + halving_scratch(n_dp, chunk),
        compiler_params=params(2),
        name="sum_back",
    )(part, first, second)


def grads_kernel(n_dp, first, second, out_first, out_second, *rest):
    greet(dp_flip_peers(n_dp))
    half = len(rest) // 2
    bits = dp_bits(n_dp)
    pair = [
        halving_of(bits[0], first, out_first, rest[:half]),
        halving_of(bits[1], second, out_second, rest[half:]),
    ]
    for one in pair:
        one.begin()
    for unit in interleaved(pair):
        unit()
    for one in pair:
        one.finish()


def grad_sums(first, second, n_dp):
    chunk = first.shape[1:]
    return pl.pallas_call(
        functools.partial(grads_kernel, n_dp),
        out_shape=(
            jax.ShapeDtypeStruct(chunk, jnp.float32),
            jax.ShapeDtypeStruct(chunk, jnp.float32),
        ),
        in_specs=[WHOLE] * 2,
        out_specs=(WHOLE,) * 2,
        scratch_shapes=halving_scratch(n_dp, chunk) + halving_scratch(n_dp, chunk),
        compiler_params=params(3),
        name="sum_grads",
    )(first, second)


def matmul(left, right, left_dim, right_dim):
    return lax.dot_general(
        left, right, (((left_dim,), (right_dim,)), ((), ())), preferred_element_type=jnp.float32
    )


def attend_kernel(spans, queries, keys, values, grads, context, d_queries, d_keys, d_values):
    scaling = DH ** (-0.5)
    wide = keys.shape[0] // spans
    for span in range(spans):
        for head in range(HEADS_AT_ONCE):
            columns = pl.ds(head * DH, DH)
            own = (pl.ds(span * SPAN, SPAN), columns)
            seen = (pl.ds(span * wide, wide), columns)
            q, g, k, v = queries[own], grads[own], keys[seen], values[seen]
            scores = matmul(q, k, 1, 1) * scaling
            weights = jnp.exp(scores - jnp.max(scores, axis=-1, keepdims=True))
            probs_wide = weights / jnp.sum(weights, axis=-1, keepdims=True)
            probs = probs_wide.astype(jnp.bfloat16)
            context[own] = matmul(probs, v, 1, 0).astype(jnp.bfloat16)
            d_probs = matmul(g, v, 1, 1)
            inner = jnp.sum(d_probs * probs_wide, axis=-1, keepdims=True)
            d_scores = (probs_wide * (d_probs - inner) * scaling).astype(jnp.bfloat16)
            d_queries[own] = matmul(d_scores, k, 1, 0).astype(jnp.bfloat16)
            d_keys[seen] = matmul(d_scores, q, 0, 0).astype(jnp.bfloat16)
            d_values[seen] = matmul(probs, g, 0, 0).astype(jnp.bfloat16)


def attend(queries, keys, values, grads, spans):
    rows, columns = queries.shape
    count = keys.shape[0]
    narrow = pl.BlockSpec((rows, DH * HEADS_AT_ONCE), lambda head: (0, head))
    tall = pl.BlockSpec((count, DH * HEADS_AT_ONCE), lambda head: (0, head))
    small = jax.ShapeDtypeStruct((rows, columns), jnp.bfloat16)
    large = jax.ShapeDtypeStruct((count, columns), jnp.bfloat16)
    return pl.pallas_call(
        functools.partial(attend_kernel, spans),
        out_shape=(small, small, large, large),
        grid=(columns // (DH * HEADS_AT_ONCE),),
        in_specs=[narrow, tall, tall, narrow],
        out_specs=(narrow, narrow, tall, tall),
        compiler_params=pltpu.CompilerParams(vmem_limit_bytes=VMEM_BYTES),
        name="attend",
    )(queries, keys, values, grads)


def per_device(queries, neighbours, targets, counts, in_weight, out_weight, kv_weight, d_context):
    length, holding, width = neighbours.shape
    n_dp, n_mp = lax.axis_size("dp"), lax.axis_size("mp")
    spans = queries.shape[0] // SPAN
    blocks = NEIGH * spans
    tokens = blocks * length
    is_live = jnp.arange(holding, dtype=jnp.int32) < counts[0]
    owners = jnp.arange(n_dp, dtype=jnp.int32)
    chosen = jnp.logical_and((targets // blocks)[None, :] == owners[:, None], is_live[None, :])
    tags = jnp.sum(jnp.where(chosen, (targets % blocks)[None, :] + 1, 0), axis=1)
    picks = chosen.astype(jnp.bfloat16)

    def picked(rows):
        return jnp.einsum("oh,thd->otd", picks, rows, preferred_element_type=jnp.float32).astype(
            jnp.bfloat16
        )

    split = max(16, length // (2 * n_mp))
    straight = length - split * n_mp
    own = lax.dynamic_slice_in_dim(
        neighbours, straight + lax.axis_index("mp") * split, split, 0
    )
    tag_rows = jnp.broadcast_to(
        tags.astype(jnp.bfloat16)[:, None, None], (n_dp, TAG_ROWS, width)
    )
    messages = [jnp.concatenate([picked(own), tag_rows], axis=1)]
    if straight:
        messages.append(picked(neighbours[:straight]))
    raw = route(messages, n_dp, n_mp, blocks, length, straight, split).reshape(tokens, width)

    normed = rms_normed(raw)
    hidden_pre = jnp.dot(normed, in_weight, preferred_element_type=jnp.float32)
    activated = gelu_value(hidden_pre).astype(jnp.bfloat16)
    part = jnp.dot(activated, out_weight, preferred_element_type=jnp.float32).astype(jnp.bfloat16)
    sliced = (CHAIN_CHUNKS, tokens // CHAIN_CHUNKS, width)
    encoded = sum_over_mp(part.reshape(sliced), raw.reshape(sliced), n_mp).reshape(tokens, width)

    key_weight, value_weight = kv_weight[:, 0], kv_weight[:, 1]
    keys = jnp.dot(encoded, key_weight, preferred_element_type=jnp.float32).astype(jnp.bfloat16)
    values = jnp.dot(encoded, value_weight, preferred_element_type=jnp.float32).astype(
        jnp.bfloat16
    )
    context, d_queries, d_keys, d_values = attend(queries, keys, values, d_context, spans)

    back = (matmul(d_keys, key_weight, 1, 1) + matmul(d_values, value_weight, 1, 1)).astype(
        jnp.bfloat16
    )
    chunked = (n_dp, width // n_dp, -1)
    key_terms = matmul(encoded, d_keys, 0, 0).astype(jnp.bfloat16).reshape(chunked)
    value_terms = matmul(encoded, d_values, 0, 0).astype(jnp.bfloat16).reshape(chunked)
    d_encoded, grad_key, grad_value = back_sums(
        back.reshape(sliced), key_terms, value_terms, n_mp, n_dp
    )
    d_encoded = d_encoded.reshape(tokens, width)

    d_act = matmul(d_encoded, out_weight, 1, 1)
    d_pre = (d_act * gelu_slope(hidden_pre)).astype(jnp.bfloat16)
    in_terms = matmul(normed, d_pre, 0, 0).astype(jnp.bfloat16).reshape(chunked)
    out_terms = matmul(d_encoded, activated, 0, 0).astype(jnp.bfloat16).reshape(chunked)
    grad_in, grad_out_t = grad_sums(in_terms, out_terms, n_dp)
    return (
        context,
        d_queries,
        jnp.stack([grad_key, grad_value], axis=1),
        grad_in,
        grad_out_t.T,
    )


def solution(mesh):
    placed = (
        P("dp", "mp"),
        P(None, "dp", None),
        P("dp"),
        P("dp"),
        P(None, "mp"),
        P("mp", None),
        P(None, None, "mp"),
        P("dp", "mp"),
    )
    return jax.shard_map(
        per_device,
        mesh=mesh,
        in_specs=placed,
        out_specs=(P("dp", "mp"), P("dp", "mp"), P("dp", None, "mp"), P("dp", "mp"), P("mp", "dp")),
        check_vma=False,
    )
```

time: 184 us -> 237 us (1.29)
  Pallas kernels: 151 us -> 203 us
    pallas_call x1, Pallas kernels: 43.3 us -> 76.3 us  [sum_over_mp(): pl.pallas_call(functools.partial(sum_kernel, n_mp), out_shape=jax.ShapeDt...]
    pallas_call x1, Pallas kernels: 45.5 us -> 77.3 us  [back_sums(): pl.pallas_call(functools.partial(back_kernel, n_mp, n_dp), out_shape=(jax...]
    pallas_call x1, Pallas kernels: 30.6 us -> 21.4 us  [route(): pl.pallas_call(functools.partial(route_kernel, n_dp, n_mp, straight, spli...]
where the time goes in v2:
time: 237 us; the launch traced here: 236 us
  Pallas kernels  203 us (86%)
  matrix products  19.3 us (8%)
  local copies, waits for them, and re-layouts  10.4 us (4%)
    pallas_call x1, Pallas kernels, back_sums(): pl.pallas_call(functools.partial(back_kernel, n_mp, n_dp), out_shape=(jax...  77.3 us
    pallas_call x1, Pallas kernels, sum_over_mp(): pl.pallas_call(functools.partial(sum_kernel, n_mp), out_shape=jax.ShapeDt...  76.3 us
    pallas_call x1, Pallas kernels, route(): pl.pallas_call(functools.partial(route_kernel, n_dp, n_mp, straight, spli...  21.4 us
    pallas_call x1, Pallas kernels, grad_sums(): pl.pallas_call(functools.partial(grads_kernel, n_dp), out_shape=(jax.Shap...  18.5 us
    dot_general x6, matrix products, matmul(): lax.dot_general(left, right, (((left_dim,), (right_dim,)), ((), ())), pre...  12.7 us
    pallas_call x1, Pallas kernels, attend(): pl.pallas_call(functools.partial(attend_kernel, spans), out_shape=(small,...  9.8 us
    slice x1, local copies, waits for them, and re-layouts, per_device(): key_weight, value_weight = (kv_weight[:, 0], kv_weight[:, 1])  5.22 us
    unnamed x21, local copies, waits for them, and re-layouts  4.97 us

profile of v2, /device:TPU:0, one launch (start us, length us, event | category | flops | bytes accessed | tf_op | source)
XLA Modules:
  0.0 236.2 jit_solution(4921455962391887778)
XLA Ops:
  0.6 0.0 copy-start
  0.6 0.0 copy-start.6
  1.5 0.7 and_select_fusion.1
  2.2 0.1 select_reduce_fusion
  2.3 0.1 broadcast_in_dim.16
  2.4 1.1 fusion.16
  3.7 0.4 fusion.13
  4.1 0.1 copy.31.refs_1_
  4.2 21.4 %route.1 = bf16[4,128,896]{2,1,0:T(8,128)(2,1)S(1)} custom-call(bf16[8,32,896]{2,1,0:T(8,128)(2,1)S(1)} %pad_maximum_fusion.1.refs_0_, bf16[8,64,896]{2,1,0:T(8,128)(2,1)S(1)} %copy.31.refs_1_), custom_call_target="tpu_custom_call" | custom-call | tf_op jit(solution)/shard_map/route/pallas_call | solution.py:388
  25.6 0.3 multiply_reduce_fusion
  25.9 0.2 fusion.7
  26.1 1.0 copy-done.5
  27.1 1.2 fusion.34
  28.3 1.3 convolution_convert_fusion.6
  29.6 76.3 %sum_encoded.1 = bf16[16,32,896]{2,1,0:T(8,128)(2,1)S(1)} custom-call(bf16[16,32,896]{2,1,0:T(8,128)(2,1)S(1)} %bitcast.57, bf16[16,32,896]{2,1,0:T(8,128)(2,1)S(1)} %bitcast.47), custom_call_target="tpu_custom_call" | custom-call | tf_op jit(solution)/shard_map/sum_encoded/pallas_call | solution.py:419
  106.0 5.2 %fusion.33 = (bf16[896,1,1024]{2,1,0:T(2,128)(2,1)S(1)}, bf16[896,1,1024]{2,1,0:T(2,128)(2,1)S(1)}) fusion(bf16[896,2,1024]{2,1,0:T(2,128)(2,1)S(1)} %copy-done.4), kind=kLoop, calls=%fused_computation.59 | loop fusion | bytes 7340032 | tf_op jit(solution)/shard_map/slice | solution.py:593
  111.2 1.3 convolution_convert_fusion.4.values
  112.5 1.3 convolution_convert_fusion.5.keys
  113.9 9.8 %attend.1 = (bf16[128,1024]{1,0:T(8,128)(2,1)}, bf16[128,1024]{1,0:T(8,128)(2,1)}, bf16[512,1024]{1,0:T(8,128)(2,1)S(1)}, bf16[512,1024]{1,0:T(8,128)(2,1)S(1)}) custom-call(bf16[128,1024]{1,0:T(8,128)(2,1)S(1)} %copy-done.1, bf16[512,1024]{1,0:T(8,128)(2,1)S(1)} %convolution_convert_fusion.5.keys, bf16[512,1024]{1,0:T(8,128)(2,1)S(1)} %convolution_convert_fusion.4.values, ...), custom_call_target="tpu_custom_call" | custom-call | tf_op jit(solution)/shard_map/attend/pallas_call | solution.py:545
  123.6 1.3 fusion.15
  125.0 1.4 add_convert_fusion
  126.3 1.1 convolution_convert_fusion.1
  127.5 1.1 convolution_convert_fusion
  128.7 77.3 %sum_back.1 = (bf16[16,32,896]{2,1,0:T(8,128)(2,1)S(1)}, f32[112,1024]{1,0:T(8,128)S(1)}, f32[112,1024]{1,0:T(8,128)S(1)}) custom-call(bf16[16,32,896]{2,1,0:T(8,128)(2,1)S(1)} %bitcast.56, bf16[8,112,1024]{2,1,0:T(8,128)(2,1)S(1)} %bitcast.48, bf16[8,112,1024]{2,1,0:T(8,128)(2,1)S(1)} %bitcast.49), custom_call_target="tpu_custom_call" | custom-call | tf_op jit(solution)/shard_map/sum_back/pallas_call | solution.py:461
  206.0 0.1 pad_maximum_fusion
  206.1 0.8 copy-done.3
  206.9 1.6 copy.20
  208.5 4.6 %convolution_convert_fusion.3 = bf16[896,896]{1,0:T(8,128)(2,1)S(1)} fusion(bf16[512,896]{1,0:T(8,128)(2,1)} %copy-done.5, f32[512,896]{1,0:T(8,128)} %copy-done.8, bf16[512,896]{1,0:T(8,128)(2,1)} %bitcast.61, bf16[896,896]{1,0:T(8,128)(2,1)S(1)} %copy-done), kind=kOutput, calls=%fused_computation.20 | convolution fusion | flops 1653686272 | bytes 6881280 | tf_op jit(solution)/shard_map/dot_general | solution.py:511
  213.2 3.0 %convolution_convert_fusion.2 = bf16[896,896]{1,0:T(8,128)(2,1)S(1)} fusion(bf16[512,896]{1,0:T(8,128)(2,1)} %bitcast.62, f32[512,896]{1,0:T(8,128)} %copy-done.8), kind=kOutput, calls=%fused_computation.19 | convolution fusion | flops 827015168 | bytes 4358144 | tf_op jit(solution)/shard_map/dot_general | solution.py:511
  216.2 18.5 %sum_grads.1 = (f32[112,896]{1,0:T(8,128)S(1)}, f32[112,896]{1,0:T(8,128)S(1)}) custom-call(bf16[8,112,896]{2,1,0:T(8,128)(2,1)S(1)} %bitcast.50, bf16[8,112,896]{2,1,0:T(8,128)(2,1)S(1)} %bitcast.51), custom_call_target="tpu_custom_call" | custom-call | tf_op jit(solution)/shard_map/sum_grads/pallas_call | solution.py:496
  234.7 0.8 copy.36
  235.5 0.7 copy.37
  (19 shorter events, 0.1 us)
Async XLA Ops:
  0.6 27.6 %copy-start = (bf16[896,896]{1,0:T(8,128)(2,1)S(1)}, bf16[896,896]{1,0:T(8,128)(2,1)}, u32[]{:S(2)}) copy-start(bf16[896,896]{1,0:T(8,128)(2,1)} %param.13) | copy-start | bytes 4816900
  0.6 3.0 %copy-start.6 = (bf16[128,8,896]{2,1,0:T(8,128)(2,1)S(1)}, bf16[128,8,896]{2,1,0:T(8,128)(2,1)}, u32[]{:S(2)}) copy-start(bf16[128,8,896]{2,1,0:T(8,128)(2,1)} %param.9) | copy-start | bytes 5505028
  25.6 1.5 copy-start.7
  26.1 1.0 copy-start.5
  28.3 1.3 copy-start.8
  28.3 77.7 %copy-start.4 = (bf16[896,2,1024]{2,1,0:T(2,128)(2,1)S(1)}, bf16[896,2,1024]{2,1,0:T(2,128)(2,1)}, u32[]{:S(2)}) copy-start(bf16[896,2,1024]{2,1,0:T(2,128)(2,1)} %param.14) | copy-start | bytes 11010052
  112.5 1.3 copy-start.1
  112.5 1.3 copy-start.2
  206.0 0.9 copy-start.3

commit v3 on v2

--- a/solution.py
+++ b/solution.py
@@ -12,10 +12,10 @@
 NEIGH = 2
 TAG_ROWS = 16
 CHAIN_CHUNKS = 16
-CHAIN_LAG = 2
+CHAIN_LAG = 7
 CHAIN_WINDOW = 4
-HEADS_AT_ONCE = 2
-VMEM_BYTES = 40 * 1024 * 1024
+HEADS_AT_ONCE = 4
+VMEM_BYTES = 24 * 1024 * 1024
 
 
 GELU_C = 0.7978845608028654
@@ -305,11 +305,11 @@
     return [flip_partner(bit)[0] for bit in range(count.bit_length() - 1)]
 
 
-def route_kernel(n_dp, n_mp, straight, split, *refs):
+def route_kernel(n_dp, n_mp, straight, split, pairs, *refs):
     if straight:
-        message, whole, out, landing, whole_landing, *sems = refs
+        message, whole, out, key_out, value_out, landing, whole_landing, *sems = refs
     else:
-        message, out, landing, *sems = refs
+        message, out, key_out, value_out, landing, *sems = refs
     greet([ring_peer("dp", step) for step in range(1, n_dp)] + mp_peers())
     blocks = out.shape[0]
     me_dp, me_mp = lax.axis_index("dp"), lax.axis_index("mp")
@@ -332,6 +332,12 @@
     if straight:
         for step in others:
             wholes(step).start()
+
+    @pl.loop(0, pairs.shape[0] // 16)
+    def _(index):
+        rows = pl.ds(pl.multiple_of(index * 16, 16), 16)
+        key_out[rows, :] = pairs[rows, 0, :]
+        value_out[rows, :] = pairs[rows, 1, :]
 
     def tags_of(rows):
         return rows.astype(jnp.float32)[:1]
@@ -383,13 +389,14 @@
         gather(step).wait_send()
 
 
-def route(messages, n_dp, n_mp, blocks, length, straight, split):
+def route(pairs, messages, n_dp, n_mp, blocks, length, straight, split):
     width = messages[0].shape[2]
+    half = jax.ShapeDtypeStruct((pairs.shape[0], pairs.shape[2]), jnp.bfloat16)
     return pl.pallas_call(
         functools.partial(route_kernel, n_dp, n_mp, straight, split),
-        out_shape=jax.ShapeDtypeStruct((blocks, length, width), jnp.bfloat16),
-        in_specs=[WHOLE] * len(messages),
-        out_specs=WHOLE,
+        out_shape=(jax.ShapeDtypeStruct((blocks, length, width), jnp.bfloat16), half, half),
+        in_specs=[WHOLE] * (1 + len(messages)),
+        out_specs=(WHOLE,) * 3,
         scratch_shapes=[
             pltpu.VMEM((n_dp - 1,) + message.shape[1:], jnp.bfloat16) for message in messages
         ]
@@ -403,7 +410,7 @@
         ],
         compiler_params=params(0),
         name="route",
-    )(*messages)
+    )(pairs, *messages)
 
 
 def sum_kernel(n_mp, part, raw, out, *scratch):
@@ -516,23 +523,31 @@
 def attend_kernel(spans, queries, keys, values, grads, context, d_queries, d_keys, d_values):
     scaling = DH ** (-0.5)
     wide = keys.shape[0] // spans
+    units = []
     for span in range(spans):
         for head in range(HEADS_AT_ONCE):
             columns = pl.ds(head * DH, DH)
-            own = (pl.ds(span * SPAN, SPAN), columns)
-            seen = (pl.ds(span * wide, wide), columns)
-            q, g, k, v = queries[own], grads[own], keys[seen], values[seen]
-            scores = matmul(q, k, 1, 1) * scaling
-            weights = jnp.exp(scores - jnp.max(scores, axis=-1, keepdims=True))
-            probs_wide = weights / jnp.sum(weights, axis=-1, keepdims=True)
-            probs = probs_wide.astype(jnp.bfloat16)
-            context[own] = matmul(probs, v, 1, 0).astype(jnp.bfloat16)
-            d_probs = matmul(g, v, 1, 1)
-            inner = jnp.sum(d_probs * probs_wide, axis=-1, keepdims=True)
-            d_scores = (probs_wide * (d_probs - inner) * scaling).astype(jnp.bfloat16)
-            d_queries[own] = matmul(d_scores, k, 1, 0).astype(jnp.bfloat16)
-            d_keys[seen] = matmul(d_scores, q, 0, 0).astype(jnp.bfloat16)
-            d_values[seen] = matmul(probs, g, 0, 0).astype(jnp.bfloat16)
+            units.append(
+                ((pl.ds(span * SPAN, SPAN), columns), (pl.ds(span * wide, wide), columns))
+            )
+    scores = [matmul(queries[own], keys[seen], 1, 1) * scaling for own, seen in units]
+    d_probs = [matmul(grads[own], values[seen], 1, 1) for own, seen in units]
+    weights = [jnp.exp(one - jnp.max(one, axis=-1, keepdims=True)) for one in scores]
+    wides = [one / jnp.sum(one, axis=-1, keepdims=True) for one in weights]
+    probs = [one.astype(jnp.bfloat16) for one in wides]
+    inners = [jnp.sum(d * p, axis=-1, keepdims=True) for d, p in zip(d_probs, wides)]
+    d_scores = [
+        (p * (d - inner) * scaling).astype(jnp.bfloat16)
+        for p, d, inner in zip(wides, d_probs, inners)
+    ]
+    for (own, seen), p in zip(units, probs):
+        context[own] = matmul(p, values[seen], 1, 0).astype(jnp.bfloat16)
+    for (own, seen), d in zip(units, d_scores):
+        d_queries[own] = matmul(d, keys[seen], 1, 0).astype(jnp.bfloat16)
+    for (own, seen), p in zip(units, probs):
+        d_values[seen] = matmul(p, grads[own], 0, 0).astype(jnp.bfloat16)
+    for (own, seen), d in zip(units, d_scores):
+        d_keys[seen] = matmul(d, queries[own], 0, 0).astype(jnp.bfloat16)
 
 
 def attend(queries, keys, values, grads, spans):
@@ -581,7 +596,10 @@
     messages = [jnp.concatenate([picked(own), tag_rows], axis=1)]
     if straight:
         messages.append(picked(neighbours[:straight]))
-    raw = route(messages, n_dp, n_mp, blocks, length, straight, split).reshape(tokens, width)
+    raw, key_weight, value_weight = route(
+        kv_weight, messages, n_dp, n_mp, blocks, length, straight, split
+    )
+    raw = raw.reshape(tokens, width)
 
     normed = rms_normed(raw)
     hidden_pre = jnp.dot(normed, in_weight, preferred_element_type=jnp.float32)
@@ -590,7 +608,6 @@
     sliced = (CHAIN_CHUNKS, tokens // CHAIN_CHUNKS, width)
     encoded = sum_over_mp(part.reshape(sliced), raw.reshape(sliced), n_mp).reshape(tokens, width)
 
-    key_weight, value_weight = kv_weight[:, 0], kv_weight[:, 1]
     keys = jnp.dot(encoded, key_weight, preferred_element_type=jnp.float32).astype(jnp.bfloat16)
     values = jnp.dot(encoded, value_weight, preferred_element_type=jnp.float32).astype(
         jnp.bfloat16

time: 237 us -> 227 us (0.958)
  Pallas kernels: 203 us -> 198 us
  local copies, waits for them, and re-layouts: 10.4 us -> 6.67 us
    pallas_call x1, Pallas kernels: 9.8 us -> 3 us  [attend(): pl.pallas_call(functools.partial(attend_kernel, spans), out_shape=(small,...]
    slice x1 -> x0, local copies, waits for them, and re-layouts: 5.22 us -> none  [per_device(): key_weight, value_weight = (kv_weight[:, 0], kv_weight[:, 1])]
    pallas_call x1, Pallas kernels: 21.4 us -> 24.7 us  [route(): pl.pallas_call(functools.partial(route_kernel, n_dp, n_mp, straight, spli...]
where the time goes in v3:
time: 227 us
  Pallas kernels  198 us (87%)
  matrix products  19.1 us (8%)
  local copies, waits for them, and re-layouts  6.67 us (3%)
    pallas_call x1, Pallas kernels, sum_over_mp(): pl.pallas_call(functools.partial(sum_kernel, n_mp), out_shape=jax.ShapeDt...  76.5 us
    pallas_call x1, Pallas kernels, back_sums(): pl.pallas_call(functools.partial(back_kernel, n_mp, n_dp), out_shape=(jax...  75.1 us
    pallas_call x1, Pallas kernels, route(): pl.pallas_call(functools.partial(route_kernel, n_dp, n_mp, straight, spli...  24.7 us
    pallas_call x1, Pallas kernels, grad_sums(): pl.pallas_call(functools.partial(grads_kernel, n_dp), out_shape=(jax.Shap...  18.4 us
    dot_general x6, matrix products, matmul(): lax.dot_general(left, right, (((left_dim,), (right_dim,)), ((), ())), pre...  12.6 us
    unnamed x21, local copies, waits for them, and re-layouts  6.41 us

profile of v3, /device:TPU:0, one launch (start us, length us, event | category | flops | bytes accessed | tf_op | source)
XLA Modules:
  0.0 226.6 jit_solution(3611000279919483566)
XLA Ops:
  0.6 0.0 copy-start
  1.5 0.7 and_select_fusion.1
  2.2 0.1 select_reduce_fusion
  2.3 0.1 broadcast_in_dim.16
  2.4 1.1 fusion.15
  3.7 0.0 copy-start.1
  3.7 0.4 fusion.13
  4.1 0.1 copy.18.refs_1_
  4.2 1.5 copy-done.1
  5.7 24.7 %route.1 = (bf16[4,128,896]{2,1,0:T(8,128)(2,1)S(1)}, bf16[896,1024]{1,0:T(8,128)(2,1)S(1)}, bf16[896,1024]{1,0:T(8,128)(2,1)S(1)}) custom-call(bf16[896,2,1024]{2,1,0:T(2,128)(2,1)S(1)} %copy-done.1, bf16[8,32,896]{2,1,0:T(8,128)(2,1)S(1)} %pad_maximum_fusion.1.refs_0_, bf16[8,64,896]{2,1,0:T(8,128)(2,1)S(1)} %copy.18.refs_1_), custom_call_target="tpu_custom_call" | custom-call | tf_op jit(solution)/shard_map/route/pallas_call | solution.py:395
  30.4 0.3 multiply_reduce_fusion
  30.6 0.2 fusion.7
  30.9 0.9 copy-done.7
  31.8 1.2 fusion.32
  33.0 1.3 convolution_convert_fusion.6
  34.3 76.5 %sum_encoded.1 = bf16[16,32,896]{2,1,0:T(8,128)(2,1)S(1)} custom-call(bf16[16,32,896]{2,1,0:T(8,128)(2,1)S(1)} %bitcast.53, bf16[16,32,896]{2,1,0:T(8,128)(2,1)S(1)} %bitcast.43), custom_call_target="tpu_custom_call" | custom-call | tf_op jit(solution)/shard_map/sum_encoded/pallas_call | solution.py:426
  110.9 1.3 convolution_convert_fusion.4.values
  112.2 1.3 convolution_convert_fusion.5.keys
  113.5 3.0 %attend.1 = (bf16[128,1024]{1,0:T(8,128)(2,1)}, bf16[128,1024]{1,0:T(8,128)(2,1)}, bf16[512,1024]{1,0:T(8,128)(2,1)S(1)}, bf16[512,1024]{1,0:T(8,128)(2,1)S(1)}) custom-call(bf16[128,1024]{1,0:T(8,128)(2,1)S(1)} %copy-done.2, bf16[512,1024]{1,0:T(8,128)(2,1)S(1)} %convolution_convert_fusion.5.keys, bf16[512,1024]{1,0:T(8,128)(2,1)S(1)} %convolution_convert_fusion.4.values, ...), custom_call_target="tpu_custom_call" | custom-call | tf_op jit(solution)/shard_map/attend/pallas_call | solution.py:560
  116.5 1.3 fusion.33
  117.7 1.3 add_convert_fusion
  119.1 1.1 convolution_convert_fusion.1
  120.2 1.1 convolution_convert_fusion
  121.4 75.1 %sum_back.1 = (bf16[16,32,896]{2,1,0:T(8,128)(2,1)S(1)}, f32[112,1024]{1,0:T(8,128)S(1)}, f32[112,1024]{1,0:T(8,128)S(1)}) custom-call(bf16[16,32,896]{2,1,0:T(8,128)(2,1)S(1)} %bitcast.52, bf16[8,112,1024]{2,1,0:T(8,128)(2,1)S(1)} %bitcast.44, bf16[8,112,1024]{2,1,0:T(8,128)(2,1)S(1)} %bitcast.45), custom_call_target="tpu_custom_call" | custom-call | tf_op jit(solution)/shard_map/sum_back/pallas_call | solution.py:468
  196.5 0.1 pad_maximum_fusion
  196.6 0.8 copy-done.4
  197.4 1.6 copy.15
  199.1 4.6 %convolution_convert_fusion.3 = bf16[896,896]{1,0:T(8,128)(2,1)S(1)} fusion(bf16[512,896]{1,0:T(8,128)(2,1)} %copy-done.5, f32[512,896]{1,0:T(8,128)} %copy-done.8, bf16[512,896]{1,0:T(8,128)(2,1)} %bitcast.57, bf16[896,896]{1,0:T(8,128)(2,1)S(1)} %copy-done), kind=kOutput, calls=%fused_computation.18 | convolution fusion | flops 1653686272 | bytes 6881280 | tf_op jit(solution)/shard_map/dot_general | solution.py:518
  203.7 3.1 %convolution_convert_fusion.2 = bf16[896,896]{1,0:T(8,128)(2,1)S(1)} fusion(bf16[512,896]{1,0:T(8,128)(2,1)} %bitcast.58, f32[512,896]{1,0:T(8,128)} %copy-done.8), kind=kOutput, calls=%fused_computation.17 | convolution fusion | flops 827015168 | bytes 4358144 | tf_op jit(solution)/shard_map/dot_general | solution.py:518
  206.8 18.4 %sum_grads.1 = (f32[112,896]{1,0:T(8,128)S(1)}, f32[112,896]{1,0:T(8,128)S(1)}) custom-call(bf16[8,112,896]{2,1,0:T(8,128)(2,1)S(1)} %bitcast.46, bf16[8,112,896]{2,1,0:T(8,128)(2,1)S(1)} %bitcast.47), custom_call_target="tpu_custom_call" | custom-call | tf_op jit(solution)/shard_map/sum_grads/pallas_call | solution.py:503
  225.1 0.8 copy.23
  225.9 0.7 copy.24
  (18 shorter events, 0.1 us)
Async XLA Ops:
  0.6 32.4 %copy-start = (bf16[896,896]{1,0:T(8,128)(2,1)S(1)}, bf16[896,896]{1,0:T(8,128)(2,1)}, u32[]{:S(2)}) copy-start(bf16[896,896]{1,0:T(8,128)(2,1)} %param.13) | copy-start | bytes 4816900
  0.6 3.0 %copy-start.6 = (bf16[128,8,896]{2,1,0:T(8,128)(2,1)S(1)}, bf16[128,8,896]{2,1,0:T(8,128)(2,1)}, u32[]{:S(2)}) copy-start(bf16[128,8,896]{2,1,0:T(8,128)(2,1)} %param.9) | copy-start | bytes 5505028
  3.7 2.0 copy-start.1
  30.4 1.4 copy-start.7
  31.8 1.2 copy-start.5
  33.0 1.3 copy-start.8
  112.2 1.3 copy-start.2
  112.2 1.3 copy-start.3
  196.5 0.9 copy-start.4

commit v4 on v3

--- a/solution.py
+++ b/solution.py
@@ -12,7 +12,8 @@
 NEIGH = 2
 TAG_ROWS = 16
 CHAIN_CHUNKS = 16
-CHAIN_LAG = 7
+ROOT_LAG = 4
+CHAIN_LAG = 8
 CHAIN_WINDOW = 4
 HEADS_AT_ONCE = 4
 VMEM_BYTES = 24 * 1024 * 1024
@@ -111,18 +112,19 @@
 
     def inner_up(self, chunk):
         root = self.root(chunk)
-        own = self.part[chunk].astype(jnp.float32)
         for toward, here in ((1, self.me < root), (-1, self.me > root)):
 
             @pl.when(here)
             def _(toward=toward):
-                total = own + self.arrived(chunk, toward)
+                total = self.part[chunk].astype(jnp.float32) + self.arrived(chunk, toward)
                 self.staged[chunk] = total.astype(jnp.bfloat16)
                 self.up(chunk, toward, self.staged).start()
 
-        @pl.when(self.me == root)
+    def inner_root(self, chunk):
+        @pl.when(self.me == self.root(chunk))
         def _():
-            total = own + self.arrived(chunk, 1) + self.arrived(chunk, -1)
+            total = self.part[chunk].astype(jnp.float32)
+            total = total + self.arrived(chunk, 1) + self.arrived(chunk, -1)
             if self.raw is not None:
                 total = total + self.raw[chunk].astype(jnp.float32)
             self.out[chunk] = total.astype(jnp.bfloat16)
@@ -157,6 +159,8 @@
         def _():
             if index < self.chunks:
                 self.inner_up(index)
+            if 0 <= index - ROOT_LAG < self.chunks:
+                self.inner_root(index - ROOT_LAG)
             if index >= CHAIN_LAG:
                 self.inner_down(index - CHAIN_LAG)
 
@@ -310,6 +314,9 @@
         message, whole, out, key_out, value_out, landing, whole_landing, *sems = refs
     else:
         message, out, key_out, value_out, landing, *sems = refs
+    *sems, pairs_here, pairs_sem = sems
+    fetch = pltpu.make_async_copy(pairs, pairs_here, pairs_sem)
+    fetch.start()
     greet([ring_peer("dp", step) for step in range(1, n_dp)] + mp_peers())
     blocks = out.shape[0]
     me_dp, me_mp = lax.axis_index("dp"), lax.axis_index("mp")
@@ -333,11 +340,13 @@
         for step in others:
             wholes(step).start()
 
+    fetch.wait()
+
     @pl.loop(0, pairs.shape[0] // 16)
     def _(index):
         rows = pl.ds(pl.multiple_of(index * 16, 16), 16)
-        key_out[rows, :] = pairs[rows, 0, :]
-        value_out[rows, :] = pairs[rows, 1, :]
+        key_out[rows, :] = pairs_here[rows, 0, :]
+        value_out[rows, :] = pairs_here[rows, 1, :]
 
     def tags_of(rows):
         return rows.astype(jnp.float32)[:1]
@@ -395,7 +404,7 @@
     return pl.pallas_call(
         functools.partial(route_kernel, n_dp, n_mp, straight, split),
         out_shape=(jax.ShapeDtypeStruct((blocks, length, width), jnp.bfloat16), half, half),
-        in_specs=[WHOLE] * (1 + len(messages)),
+        in_specs=[pl.BlockSpec(memory_space=pltpu.HBM)] + [WHOLE] * len(messages),
         out_specs=(WHOLE,) * 3,
         scratch_shapes=[
             pltpu.VMEM((n_dp - 1,) + message.shape[1:], jnp.bfloat16) for message in messages
@@ -407,6 +416,8 @@
             pltpu.SemaphoreType.DMA((n_mp - 1,)),
             pltpu.SemaphoreType.DMA((n_dp - 1,)),
             pltpu.SemaphoreType.DMA((n_dp - 1,)),
+            pltpu.VMEM(pairs.shape, jnp.bfloat16),
+            pltpu.SemaphoreType.DMA,
         ],
         compiler_params=params(0),
         name="route",
@@ -453,7 +464,7 @@
     units = interleaved(pair)
     for index in range(total.steps):
         total.step(index)
-        if index > 0 and units:
+        if index > 1 and units:
             units.pop(0)()
     for unit in units:
         unit()

time: 227 us -> 147 us (0.65)
  Pallas kernels: 198 us -> 118 us
    pallas_call x1, Pallas kernels: 75.1 us -> 35.1 us  [back_sums(): pl.pallas_call(functools.partial(back_kernel, n_mp, n_dp), out_shape=(jax...]
    pallas_call x1, Pallas kernels: 76.5 us -> 36.5 us  [sum_over_mp(): pl.pallas_call(functools.partial(sum_kernel, n_mp), out_shape=jax.ShapeDt...]
where the time goes in v4:
time: 147 us
  Pallas kernels  118 us (80%)
  matrix products  19.1 us (13%)
  local copies, waits for them, and re-layouts  6.67 us (5%)
  between operations  1.72 us (1%)
  other arithmetic  1.48 us (1%)
    pallas_call x1, Pallas kernels, sum_over_mp(): pl.pallas_call(functools.partial(sum_kernel, n_mp), out_shape=jax.ShapeDt...  36.5 us
    pallas_call x1, Pallas kernels, back_sums(): pl.pallas_call(functools.partial(back_kernel, n_mp, n_dp), out_shape=(jax...  35.1 us
    pallas_call x1, Pallas kernels, route(): pl.pallas_call(functools.partial(route_kernel, n_dp, n_mp, straight, spli...  24.9 us
    pallas_call x1, Pallas kernels, grad_sums(): pl.pallas_call(functools.partial(grads_kernel, n_dp), out_shape=(jax.Shap...  18.3 us
    dot_general x6, matrix products, matmul(): lax.dot_general(left, right, (((left_dim,), (right_dim,)), ((), ())), pre...  12.6 us
    unnamed x21, local copies, waits for them, and re-layouts  6.41 us
    pallas_call x1, Pallas kernels, attend(): pl.pallas_call(functools.partial(attend_kernel, spans), out_shape=(small,...  3 us

profile of v4, /device:TPU:0, one launch (start us, length us, event | category | flops | bytes accessed | tf_op | source)
XLA Modules:
  0.0 146.8 jit_solution(10879070727156923014)
XLA Ops:
  0.6 0.0 copy-start
  1.5 0.7 and_select_fusion.1
  2.2 0.1 select_reduce_fusion
  2.3 0.1 broadcast_in_dim.16
  2.4 1.1 fusion.15
  3.7 0.0 copy-start.1
  3.7 0.4 fusion.13
  4.1 0.1 copy.18.refs_1_
  4.2 1.5 %copy-done.1 = bf16[896,2,1024]{2,1,0:T(2,128)(2,1)S(1)} copy-done((bf16[896,2,1024]{2,1,0:T(2,128)(2,1)S(1)}, bf16[896,2,1024]{2,1,0:T(2,128)(2,1)}, u32[]{:S(2)}) %copy-start.1) | copy-done | bytes 3670040
  5.7 24.9 %route.1 = (bf16[4,128,896]{2,1,0:T(8,128)(2,1)S(1)}, bf16[896,1024]{1,0:T(8,128)(2,1)S(1)}, bf16[896,1024]{1,0:T(8,128)(2,1)S(1)}) custom-call(bf16[896,2,1024]{2,1,0:T(2,128)(2,1)S(1)} %copy-done.1, bf16[8,32,896]{2,1,0:T(8,128)(2,1)S(1)} %pad_maximum_fusion.1.refs_0_, bf16[8,64,896]{2,1,0:T(8,128)(2,1)S(1)} %copy.18.refs_1_), custom_call_target="tpu_custom_call" | custom-call | tf_op jit(solution)/shard_map/route/pallas_call | solution.py:404
  30.7 0.3 multiply_reduce_fusion
  30.9 0.2 fusion.7
  31.2 0.9 copy-done.7
  32.1 1.2 fusion.32
  33.3 1.3 convolution_convert_fusion.6
  34.6 36.5 %sum_encoded.1 = bf16[16,32,896]{2,1,0:T(8,128)(2,1)S(1)} custom-call(bf16[16,32,896]{2,1,0:T(8,128)(2,1)S(1)} %bitcast.53, bf16[16,32,896]{2,1,0:T(8,128)(2,1)S(1)} %bitcast.43), custom_call_target="tpu_custom_call" | custom-call | tf_op jit(solution)/shard_map/sum_encoded/pallas_call | solution.py:437
  71.2 1.3 convolution_convert_fusion.4.values
  72.5 1.3 convolution_convert_fusion.5.keys
  73.7 3.0 %attend.1 = (bf16[128,1024]{1,0:T(8,128)(2,1)}, bf16[128,1024]{1,0:T(8,128)(2,1)}, bf16[512,1024]{1,0:T(8,128)(2,1)S(1)}, bf16[512,1024]{1,0:T(8,128)(2,1)S(1)}) custom-call(bf16[128,1024]{1,0:T(8,128)(2,1)S(1)} %copy-done.2, bf16[512,1024]{1,0:T(8,128)(2,1)S(1)} %convolution_convert_fusion.5.keys, bf16[512,1024]{1,0:T(8,128)(2,1)S(1)} %convolution_convert_fusion.4.values, ...), custom_call_target="tpu_custom_call" | custom-call | tf_op jit(solution)/shard_map/attend/pallas_call | solution.py:571
  76.7 1.3 fusion.33
  78.0 1.3 add_convert_fusion
  79.3 1.1 convolution_convert_fusion.1
  80.5 1.1 convolution_convert_fusion
  81.6 35.1 %sum_back.1 = (bf16[16,32,896]{2,1,0:T(8,128)(2,1)S(1)}, f32[112,1024]{1,0:T(8,128)S(1)}, f32[112,1024]{1,0:T(8,128)S(1)}) custom-call(bf16[16,32,896]{2,1,0:T(8,128)(2,1)S(1)} %bitcast.52, bf16[8,112,1024]{2,1,0:T(8,128)(2,1)S(1)} %bitcast.44, bf16[8,112,1024]{2,1,0:T(8,128)(2,1)S(1)} %bitcast.45), custom_call_target="tpu_custom_call" | custom-call | tf_op jit(solution)/shard_map/sum_back/pallas_call | solution.py:479
  116.7 0.1 pad_maximum_fusion
  116.8 0.8 copy-done.4
  117.7 1.6 %copy.15 = f32[112,2,1024]{2,1,0:T(2,128)} copy(f32[112,2,1024]{2,0,1:T(8,128)S(1)} %pad_maximum_fusion) | data formatting | bytes 1835008
  119.3 4.6 %convolution_convert_fusion.3 = bf16[896,896]{1,0:T(8,128)(2,1)S(1)} fusion(bf16[512,896]{1,0:T(8,128)(2,1)} %copy-done.5, f32[512,896]{1,0:T(8,128)} %copy-done.8, bf16[512,896]{1,0:T(8,128)(2,1)} %bitcast.57, bf16[896,896]{1,0:T(8,128)(2,1)S(1)} %copy-done), kind=kOutput, calls=%fused_computation.18 | convolution fusion | flops 1653686272 | bytes 6881280 | tf_op jit(solution)/shard_map/dot_general | solution.py:529
  123.9 3.1 %convolution_convert_fusion.2 = bf16[896,896]{1,0:T(8,128)(2,1)S(1)} fusion(bf16[512,896]{1,0:T(8,128)(2,1)} %bitcast.58, f32[512,896]{1,0:T(8,128)} %copy-done.8), kind=kOutput, calls=%fused_computation.17 | convolution fusion | flops 827015168 | bytes 4358144 | tf_op jit(solution)/shard_map/dot_general | solution.py:529
  127.0 18.3 %sum_grads.1 = (f32[112,896]{1,0:T(8,128)S(1)}, f32[112,896]{1,0:T(8,128)S(1)}) custom-call(bf16[8,112,896]{2,1,0:T(8,128)(2,1)S(1)} %bitcast.46, bf16[8,112,896]{2,1,0:T(8,128)(2,1)S(1)} %bitcast.47), custom_call_target="tpu_custom_call" | custom-call | tf_op jit(solution)/shard_map/sum_grads/pallas_call | solution.py:514
  145.3 0.8 copy.23
  146.0 0.7 copy.24
  (18 shorter events, 0.1 us)
Async XLA Ops:
  0.6 32.7 %copy-start = (bf16[896,896]{1,0:T(8,128)(2,1)S(1)}, bf16[896,896]{1,0:T(8,128)(2,1)}, u32[]{:S(2)}) copy-start(bf16[896,896]{1,0:T(8,128)(2,1)} %param.13) | copy-start | bytes 4816900
  0.6 3.0 %copy-start.6 = (bf16[128,8,896]{2,1,0:T(8,128)(2,1)S(1)}, bf16[128,8,896]{2,1,0:T(8,128)(2,1)}, u32[]{:S(2)}) copy-start(bf16[128,8,896]{2,1,0:T(8,128)(2,1)} %param.9) | copy-start | bytes 5505028
  3.7 2.0 %copy-start.1 = (bf16[896,2,1024]{2,1,0:T(2,128)(2,1)S(1)}, bf16[896,2,1024]{2,1,0:T(2,128)(2,1)}, u32[]{:S(2)}) copy-start(bf16[896,2,1024]{2,1,0:T(2,128)(2,1)} %pairs.1) | copy-start | bytes 11010052
  30.7 1.4 copy-start.7
  32.1 1.2 copy-start.5
  33.3 1.3 copy-start.8
  72.4 1.3 copy-start.2
  72.5 1.3 copy-start.3
  116.7 0.9 copy-start.4

commit v5 on v4

--- a/solution.py
+++ b/solution.py
@@ -11,6 +11,7 @@
 SPAN = 64
 NEIGH = 2
 TAG_ROWS = 16
+LANES = 128
 CHAIN_CHUNKS = 16
 ROOT_LAG = 4
 CHAIN_LAG = 8
@@ -311,9 +312,9 @@
 
 def route_kernel(n_dp, n_mp, straight, split, pairs, *refs):
     if straight:
-        message, whole, out, key_out, value_out, landing, whole_landing, *sems = refs
+        labels, message, whole, out, key_out, value_out, labels_in, landing, whole_landing, *sems = refs
     else:
-        message, out, key_out, value_out, landing, *sems = refs
+        labels, message, out, key_out, value_out, labels_in, landing, *sems = refs
     *sems, pairs_here, pairs_sem = sems
     fetch = pltpu.make_async_copy(pairs, pairs_here, pairs_sem)
     fetch.start()
@@ -333,8 +334,12 @@
     def wholes(step):
         return exchange(whole, whole_landing, step, sems[4], sems[5])
 
+    def marks(step):
+        return exchange(labels, labels_in, step, sems[6], sems[7])
+
     others = range(1, n_dp)
     for step in others:
+        marks(step).start()
         parts(step).start()
     if straight:
         for step in others:
@@ -349,15 +354,13 @@
         value_out[rows, :] = pairs_here[rows, 1, :]
 
     def tags_of(rows):
-        return rows.astype(jnp.float32)[:1]
+        return jnp.concatenate([rows.astype(jnp.float32)[:1]] * (out.shape[2] // LANES), axis=1)
 
     for step in others:
+        marks(step).wait_recv()
         parts(step).wait_recv()
     data_rows = pl.ds(0, split)
-    tag_rows = pl.ds(split, TAG_ROWS)
-    tags = [tags_of(message[me_dp, tag_rows])] + [
-        tags_of(landing[step - 1, tag_rows]) for step in others
-    ]
+    tags = [tags_of(labels[me_dp])] + [tags_of(labels_in[step - 1]) for step in others]
 
     def place(own, arrived, first, where):
         sources = [own[me_dp, first]] + [arrived[step - 1, first] for step in others]
@@ -391,6 +394,7 @@
     for step in range(1, n_mp):
         gather(step).wait_recv()
     for step in others:
+        marks(step).wait_send()
         parts(step).wait_send()
         if straight:
             wholes(step).wait_send()
@@ -399,7 +403,7 @@
 
 
 def route(pairs, messages, n_dp, n_mp, blocks, length, straight, split):
-    width = messages[0].shape[2]
+    width = messages[1].shape[2]
     half = jax.ShapeDtypeStruct((pairs.shape[0], pairs.shape[2]), jnp.bfloat16)
     return pl.pallas_call(
         functools.partial(route_kernel, n_dp, n_mp, straight, split),
@@ -416,6 +420,8 @@
             pltpu.SemaphoreType.DMA((n_mp - 1,)),
             pltpu.SemaphoreType.DMA((n_dp - 1,)),
             pltpu.SemaphoreType.DMA((n_dp - 1,)),
+            pltpu.SemaphoreType.DMA((n_dp - 1,)),
+            pltpu.SemaphoreType.DMA((n_dp - 1,)),
             pltpu.VMEM(pairs.shape, jnp.bfloat16),
             pltpu.SemaphoreType.DMA,
         ],
@@ -424,40 +430,45 @@
     )(pairs, *messages)
 
 
-def sum_kernel(n_mp, part, raw, out, *scratch):
+def sum_kernel(n_mp, part, raw, hidden, out, slope, *scratch):
     greet(mp_peers())
     total = ChainOverMp(n_mp, part, raw, out, scratch)
     for index in range(total.steps):
         total.step(index)
+        if index < total.chunks:
+            slope[index] = gelu_slope(hidden[index])
     total.finish()
 
 
-def sum_over_mp(part, raw, n_mp):
+def sum_over_mp(part, raw, hidden, n_mp):
     rows, width = part.shape[1:]
     return pl.pallas_call(
         functools.partial(sum_kernel, n_mp),
-        out_shape=jax.ShapeDtypeStruct(part.shape, jnp.bfloat16),
-        in_specs=[WHOLE, WHOLE],
-        out_specs=WHOLE,
+        out_shape=(
+            jax.ShapeDtypeStruct(part.shape, jnp.bfloat16),
+            jax.ShapeDtypeStruct(hidden.shape, jnp.float32),
+        ),
+        in_specs=[WHOLE] * 3,
+        out_specs=(WHOLE,) * 2,
         scratch_shapes=mp_scratch(part.shape[0], rows, width),
         compiler_params=params(1),
         name="sum_encoded",
-    )(part, raw)
+    )(part, raw, hidden)
 
 
 def interleaved(pair):
     return [unit for both in zip(*(one.units() for one in pair)) for unit in both]
 
 
-def back_kernel(n_mp, n_dp, part, first, second, out, out_first, out_second, *rest):
+def back_kernel(n_mp, n_dp, part, first, second, out, out_pair, *rest):
     greet(mp_peers() + dp_flip_peers(n_dp))
     chain, rest = rest[:6], rest[6:]
     half = len(rest) // 2
     bits = dp_bits(n_dp)
     total = ChainOverMp(n_mp, part, None, out, chain)
     pair = [
-        halving_of(bits[0], first, out_first, rest[:half]),
-        halving_of(bits[1], second, out_second, rest[half:]),
+        halving_of(bits[0], first, out_pair.at[:, 0], rest[:half]),
+        halving_of(bits[1], second, out_pair.at[:, 1], rest[half:]),
     ]
     for one in pair:
         one.begin()
@@ -480,11 +491,10 @@
         functools.partial(back_kernel, n_mp, n_dp),
         out_shape=(
             jax.ShapeDtypeStruct(part.shape, jnp.bfloat16),
-            jax.ShapeDtypeStruct(chunk, jnp.float32),
-            jax.ShapeDtypeStruct(chunk, jnp.float32),
+            jax.ShapeDtypeStruct((chunk[0], 2, chunk[1]), jnp.float32),
         ),
         in_specs=[WHOLE] * 3,
-        out_specs=(WHOLE,) * 3,
+        out_specs=(WHOLE,) * 2,
         scratch_shapes=mp_scratch(part.shape[0], rows, width)
         + halving_scratch(n_dp, chunk)
         + halving_scratch(n_dp, chunk),
@@ -602,9 +612,9 @@
         neighbours, straight + lax.axis_index("mp") * split, split, 0
     )
     tag_rows = jnp.broadcast_to(
-        tags.astype(jnp.bfloat16)[:, None, None], (n_dp, TAG_ROWS, width)
-    )
-    messages = [jnp.concatenate([picked(own), tag_rows], axis=1)]
+        tags.astype(jnp.bfloat16)[:, None, None], (n_dp, TAG_ROWS, LANES)
+    )
+    messages = [tag_rows, picked(own)]
     if straight:
         messages.append(picked(neighbours[:straight]))
     raw, key_weight, value_weight = route(
@@ -614,10 +624,16 @@
 
     normed = rms_normed(raw)
     hidden_pre = jnp.dot(normed, in_weight, preferred_element_type=jnp.float32)
-    activated = gelu_value(hidden_pre).astype(jnp.bfloat16)
+    activated = lax.optimization_barrier(gelu_value(hidden_pre).astype(jnp.bfloat16))
     part = jnp.dot(activated, out_weight, preferred_element_type=jnp.float32).astype(jnp.bfloat16)
     sliced = (CHAIN_CHUNKS, tokens // CHAIN_CHUNKS, width)
-    encoded = sum_over_mp(part.reshape(sliced), raw.reshape(sliced), n_mp).reshape(tokens, width)
+    encoded, slope = sum_over_mp(
+        part.reshape(sliced),
+        raw.reshape(sliced),
+        hidden_pre.reshape(CHAIN_CHUNKS, tokens // CHAIN_CHUNKS, -1),
+        n_mp,
+    )
+    encoded = encoded.reshape(tokens, width)
 
     keys = jnp.dot(encoded, key_weight, preferred_element_type=jnp.float32).astype(jnp.bfloat16)
     values = jnp.dot(encoded, value_weight, preferred_element_type=jnp.float32).astype(
@@ -631,20 +647,20 @@
     chunked = (n_dp, width // n_dp, -1)
     key_terms = matmul(encoded, d_keys, 0, 0).astype(jnp.bfloat16).reshape(chunked)
     value_terms = matmul(encoded, d_values, 0, 0).astype(jnp.bfloat16).reshape(chunked)
-    d_encoded, grad_key, grad_value = back_sums(
+    d_encoded, grad_kv = back_sums(
         back.reshape(sliced), key_terms, value_terms, n_mp, n_dp
     )
     d_encoded = d_encoded.reshape(tokens, width)
 
     d_act = matmul(d_encoded, out_weight, 1, 1)
-    d_pre = (d_act * gelu_slope(hidden_pre)).astype(jnp.bfloat16)
+    d_pre = (d_act * slope.reshape(d_act.shape)).astype(jnp.bfloat16)
     in_terms = matmul(normed, d_pre, 0, 0).astype(jnp.bfloat16).reshape(chunked)
     out_terms = matmul(d_encoded, activated, 0, 0).astype(jnp.bfloat16).reshape(chunked)
     grad_in, grad_out_t = grad_sums(in_terms, out_terms, n_dp)
     return (
         context,
         d_queries,
-        jnp.stack([grad_key, grad_value], axis=1),
+        grad_kv,
         grad_in,
         grad_out_t.T,
     )

time: 147 us -> 140 us (0.952)
  local copies, waits for them, and re-layouts: 6.67 us -> 3.14 us
  matrix products: 19.1 us -> 16.3 us
    dot_general x6 -> x7, matrix products: 12.6 us -> 8.38 us  [matmul(): lax.dot_general(left, right, (((left_dim,), (right_dim,)), ((), ())), pre...]
    unnamed x21 -> x13, local copies, waits for them, and re-layouts: 6.41 us -> 2.9 us
where the time goes in v5:
time: 140 us
  Pallas kernels  118 us (84%)
  matrix products  16.3 us (12%)
  local copies, waits for them, and re-layouts  3.14 us (2%)
  between operations  1.62 us (1%)
    pallas_call x1, Pallas kernels, sum_over_mp(): pl.pallas_call(functools.partial(sum_kernel, n_mp), out_shape=(jax.ShapeD...  36.8 us
    pallas_call x1, Pallas kernels, back_sums(): pl.pallas_call(functools.partial(back_kernel, n_mp, n_dp), out_shape=(jax...  34.2 us
    pallas_call x1, Pallas kernels, route(): pl.pallas_call(functools.partial(route_kernel, n_dp, n_mp, straight, spli...  24.9 us
    pallas_call x1, Pallas kernels, grad_sums(): pl.pallas_call(functools.partial(grads_kernel, n_dp), out_shape=(jax.Shap...  18.9 us
    dot_general x7, matrix products, matmul(): lax.dot_general(left, right, (((left_dim,), (right_dim,)), ((), ())), pre...  8.38 us
    pallas_call x1, Pallas kernels, attend(): pl.pallas_call(functools.partial(attend_kernel, spans), out_shape=(small,...  3 us
    unnamed x13, local copies, waits for them, and re-layouts  2.9 us
    dot_general x2, matrix products, picked(): jnp.einsum('oh,thd->otd', picks, rows, preferred_element_type=jnp.float32)  2.86 us

profile of v5, /device:TPU:0, one launch (start us, length us, event | category | flops | bytes accessed | tf_op | source)
XLA Modules:
  0.0 140.1 jit_solution(15178577130602325657)
XLA Ops:
  0.6 0.0 copy-start
  1.4 0.7 and_select_fusion.1
  2.1 0.1 select_reduce_fusion
  2.2 0.1 broadcast_in_dim.16.refs_0_
  2.3 1.1 fusion.9
  3.5 0.0 copy-start.1
  3.5 1.7 %fusion.7 = bf16[8,64,896]{2,0,1:T(8,128)(2,1)S(1)} fusion(bf16[128,8,896]{2,1,0:T(8,128)(2,1)} %param.9, s32[8]{0:T(128)S(1)} %get-tuple-element.31, pred[8]{0:T(512)(128)(4,1)S(1)} %iota_compare_fusion.1), kind=kOutput, calls=%fused_computation.20 | convolution fusion | flops 7340160 | bytes 1835048 | tf_op jit(solution)/shard_map/oh,thd->otd/dot_general | solution.py:605
  5.2 0.1 copy.17.refs_2_
  5.4 0.4 copy-done.1
  5.8 24.9 %route.1 = (bf16[4,128,896]{2,1,0:T(8,128)(2,1)S(1)}, bf16[896,1024]{1,0:T(8,128)(2,1)S(1)}, bf16[896,1024]{1,0:T(8,128)(2,1)S(1)}) custom-call(bf16[896,2,1024]{2,1,0:T(2,128)(2,1)S(1)} %copy-done.1, bf16[8,16,128]{2,1,0:T(8,128)(2,1)S(1)} %broadcast_in_dim.16.refs_0_, bf16[8,16,896]{2,1,0:T(8,128)(2,1)S(1)} %copy.18.refs_1_, ...), custom_call_target="tpu_custom_call" | custom-call | tf_op jit(solution)/shard_map/route/pallas_call | solution.py:408
  30.7 0.3 multiply_reduce_fusion
  31.0 0.2 fusion.6
  31.2 0.0 copy-start.4
  31.3 1.4 fusion.4
  32.6 0.0 copy-done.4
  32.7 1.2 convolution_convert_fusion.6
  33.9 36.8 %sum_encoded.1 = (bf16[16,32,896]{2,1,0:T(8,128)(2,1)S(1)}, f32[16,32,896]{2,1,0:T(8,128)S(1)}) custom-call(bf16[16,32,896]{2,1,0:T(8,128)(2,1)S(1)} %bitcast.57, bf16[16,32,896]{2,1,0:T(8,128)(2,1)S(1)} %bitcast.49, f32[16,32,896]{2,1,0:T(8,128)S(1)} %bitcast.51), custom_call_target="tpu_custom_call" | custom-call | tf_op jit(solution)/shard_map/sum_encoded/pallas_call | solution.py:445
  70.6 1.3 convolution_convert_fusion.4.values
  71.9 1.3 convolution_convert_fusion.5.keys
  73.2 3.0 %attend.1 = (bf16[128,1024]{1,0:T(8,128)(2,1)}, bf16[128,1024]{1,0:T(8,128)(2,1)}, bf16[512,1024]{1,0:T(8,128)(2,1)S(1)}, bf16[512,1024]{1,0:T(8,128)(2,1)S(1)}) custom-call(bf16[128,1024]{1,0:T(8,128)(2,1)S(1)} %copy-done.2, bf16[512,1024]{1,0:T(8,128)(2,1)S(1)} %convolution_convert_fusion.5.keys, bf16[512,1024]{1,0:T(8,128)(2,1)S(1)} %convolution_convert_fusion.4.values, ...), custom_call_target="tpu_custom_call" | custom-call | tf_op jit(solution)/shard_map/attend/pallas_call | solution.py:581
  76.2 1.3 fusion.21
  77.5 1.3 add_convert_fusion
  78.8 1.1 convolution_convert_fusion.1
  79.9 1.1 convolution_convert_fusion
  81.1 34.2 %sum_back.1 = (bf16[16,32,896]{2,1,0:T(8,128)(2,1)S(1)}, f32[112,2,1024]{2,1,0:T(2,128)S(1)}) custom-call(bf16[16,32,896]{2,1,0:T(8,128)(2,1)S(1)} %bitcast.58, bf16[8,112,1024]{2,1,0:T(8,128)(2,1)S(1)} %bitcast.50, bf16[8,112,1024]{2,1,0:T(8,128)(2,1)S(1)} %bitcast.52), custom_call_target="tpu_custom_call" | custom-call | tf_op jit(solution)/shard_map/sum_back/pallas_call | solution.py:490
  115.3 1.2 fusion.5
  116.5 1.1 convolution_convert_fusion.2
  117.7 1.1 convolution_convert_fusion.3
  118.8 18.9 %sum_grads.1 = (f32[112,896]{1,0:T(8,128)S(1)}, f32[112,896]{1,0:T(8,128)S(1)}) custom-call(bf16[8,112,896]{2,1,0:T(8,128)(2,1)S(1)} %bitcast.54, bf16[8,112,896]{2,1,0:T(8,128)(2,1)S(1)} %bitcast.53), custom_call_target="tpu_custom_call" | custom-call | tf_op jit(solution)/shard_map/sum_grads/pallas_call | solution.py:524
  137.7 0.9 copy.23
  138.6 0.7 copy.24
  139.4 0.7 copy.25
  (9 shorter events, 0.1 us)
Async XLA Ops:
  0.6 30.6 %copy-start = (bf16[896,896]{1,0:T(8,128)(2,1)S(1)}, bf16[896,896]{1,0:T(8,128)(2,1)}, u32[]{:S(2)}) copy-start(bf16[896,896]{1,0:T(8,128)(2,1)} %param.12) | copy-start | bytes 4816900
  3.5 2.3 %copy-start.1 = (bf16[896,2,1024]{2,1,0:T(2,128)(2,1)S(1)}, bf16[896,2,1024]{2,1,0:T(2,128)(2,1)}, u32[]{:S(2)}) copy-start(bf16[896,2,1024]{2,1,0:T(2,128)(2,1)} %pairs.1) | copy-start | bytes 11010052
  31.2 1.4 %copy-start.4 = (bf16[896,896]{1,0:T(8,128)(2,1)S(1)}, bf16[896,896]{1,0:T(8,128)(2,1)}, u32[]{:S(2)}) copy-start(bf16[896,896]{1,0:T(8,128)(2,1)} %param.13) | copy-start | bytes 4816900
  71.9 1.3 copy-start.2
  71.9 1.3 copy-start.3

commit v6 on v5

--- a/solution.py
+++ b/solution.py
@@ -12,10 +12,10 @@
 NEIGH = 2
 TAG_ROWS = 16
 LANES = 128
-CHAIN_CHUNKS = 16
-ROOT_LAG = 4
-CHAIN_LAG = 8
-CHAIN_WINDOW = 4
+CHAIN_CHUNKS = 32
+ROOT_LAG = 6
+CHAIN_LAG = 12
+CHAIN_WINDOW = 8
 HEADS_AT_ONCE = 4
 VMEM_BYTES = 24 * 1024 * 1024
 
@@ -345,14 +345,6 @@
         for step in others:
             wholes(step).start()
 
-    fetch.wait()
-
-    @pl.loop(0, pairs.shape[0] // 16)
-    def _(index):
-        rows = pl.ds(pl.multiple_of(index * 16, 16), 16)
-        key_out[rows, :] = pairs_here[rows, 0, :]
-        value_out[rows, :] = pairs_here[rows, 1, :]
-
     def tags_of(rows):
         return jnp.concatenate([rows.astype(jnp.float32)[:1]] * (out.shape[2] // LANES), axis=1)
 
@@ -385,6 +377,14 @@
 
     for step in range(1, n_mp):
         gather(step).start()
+    fetch.wait()
+
+    @pl.loop(0, pairs.shape[0] // 16)
+    def _(index):
+        rows = pl.ds(pl.multiple_of(index * 16, 16), 16)
+        key_out[rows, :] = pairs_here[rows, 0, :]
+        value_out[rows, :] = pairs_here[rows, 1, :]
+
     if straight:
         for step in others:
             wholes(step).wait_recv()

time: 140 us -> 144 us (1.029)
  Pallas kernels: 118 us -> 122 us
    pallas_call x1, Pallas kernels: 34.2 us -> 46.9 us  [back_sums(): pl.pallas_call(functools.partial(back_kernel, n_mp, n_dp), out_shape=(jax...]
    pallas_call x1, Pallas kernels: 24.9 us -> 20.9 us  [route(): pl.pallas_call(functools.partial(route_kernel, n_dp, n_mp, straight, spli...]
    pallas_call x1, Pallas kernels: 36.8 us -> 33.3 us  [sum_over_mp(): pl.pallas_call(functools.partial(sum_kernel, n_mp), out_shape=(jax.ShapeD...]
where the time goes in v6:
time: 144 us
  Pallas kernels  122 us (85%)
  matrix products  16.3 us (11%)
  local copies, waits for them, and re-layouts  3.14 us (2%)
  between operations  1.62 us (1%)
    pallas_call x1, Pallas kernels, back_sums(): pl.pallas_call(functools.partial(back_kernel, n_mp, n_dp), out_shape=(jax...  46.9 us
    pallas_call x1, Pallas kernels, sum_over_mp(): pl.pallas_call(functools.partial(sum_kernel, n_mp), out_shape=(jax.ShapeD...  33.3 us
    pallas_call x1, Pallas kernels, route(): pl.pallas_call(functools.partial(route_kernel, n_dp, n_mp, straight, spli...  20.9 us
    pallas_call x1, Pallas kernels, grad_sums(): pl.pallas_call(functools.partial(grads_kernel, n_dp), out_shape=(jax.Shap...  17.6 us
    dot_general x7, matrix products, matmul(): lax.dot_general(left, right, (((left_dim,), (right_dim,)), ((), ())), pre...  8.38 us
    pallas_call x1, Pallas kernels, attend(): pl.pallas_call(functools.partial(attend_kernel, spans), out_shape=(small,...  3 us
    unnamed x13, local copies, waits for them, and re-layouts  2.9 us

profile of v6, /device:TPU:0, one launch (start us, length us, event | category | flops | bytes accessed | tf_op | source)
XLA Modules:
  0.0 144.1 jit_solution(8059578870767108652)
XLA Ops:
  0.6 0.0 copy-start
  1.4 0.7 and_select_fusion.1
  2.1 0.1 select_reduce_fusion
  2.2 0.1 broadcast_in_dim.16.refs_0_
  2.3 1.1 fusion.9
  3.5 1.7 %fusion.7 = bf16[8,64,896]{2,0,1:T(8,128)(2,1)S(1)} fusion(bf16[128,8,896]{2,1,0:T(8,128)(2,1)} %param.9, s32[8]{0:T(128)S(1)} %get-tuple-element.31, pred[8]{0:T(512)(128)(4,1)S(1)} %iota_compare_fusion.1), kind=kOutput, calls=%fused_computation.20 | convolution fusion | flops 7340160 | bytes 1835048 | tf_op jit(solution)/shard_map/oh,thd->otd/dot_general | solution.py:605
  5.2 0.1 copy.17.refs_2_
  5.4 0.4 copy-done.1
  5.8 20.9 %route.1 = (bf16[4,128,896]{2,1,0:T(8,128)(2,1)S(1)}, bf16[896,1024]{1,0:T(8,128)(2,1)S(1)}, bf16[896,1024]{1,0:T(8,128)(2,1)S(1)}) custom-call(bf16[896,2,1024]{2,1,0:T(2,128)(2,1)S(1)} %copy-done.1, bf16[8,16,128]{2,1,0:T(8,128)(2,1)S(1)} %broadcast_in_dim.16.refs_0_, bf16[8,16,896]{2,1,0:T(8,128)(2,1)S(1)} %copy.18.refs_1_, ...), custom_call_target="tpu_custom_call" | custom-call | tf_op jit(solution)/shard_map/route/pallas_call | solution.py:408
  26.7 0.3 multiply_reduce_fusion
  26.9 0.2 fusion.6
  27.2 1.4 fusion.4
  28.6 0.0 copy-done.4
  28.6 1.2 convolution_convert_fusion.6
  29.8 33.3 %sum_encoded.1 = (bf16[32,16,896]{2,1,0:T(8,128)(2,1)S(1)}, f32[32,16,896]{2,1,0:T(8,128)S(1)}) custom-call(bf16[32,16,896]{2,1,0:T(8,128)(2,1)S(1)} %bitcast.57, bf16[32,16,896]{2,1,0:T(8,128)(2,1)S(1)} %bitcast.49, f32[32,16,896]{2,1,0:T(8,128)S(1)} %bitcast.51), custom_call_target="tpu_custom_call" | custom-call | tf_op jit(solution)/shard_map/sum_encoded/pallas_call | solution.py:445
  63.1 1.3 convolution_convert_fusion.4.values
  64.3 0.0 copy-start.2
  64.4 0.0 copy-start.3
  64.4 1.3 convolution_convert_fusion.5.keys
  65.7 3.0 %attend.1 = (bf16[128,1024]{1,0:T(8,128)(2,1)}, bf16[128,1024]{1,0:T(8,128)(2,1)}, bf16[512,1024]{1,0:T(8,128)(2,1)S(1)}, bf16[512,1024]{1,0:T(8,128)(2,1)S(1)}) custom-call(bf16[128,1024]{1,0:T(8,128)(2,1)S(1)} %copy-done.2, bf16[512,1024]{1,0:T(8,128)(2,1)S(1)} %convolution_convert_fusion.5.keys, bf16[512,1024]{1,0:T(8,128)(2,1)S(1)} %convolution_convert_fusion.4.values, ...), custom_call_target="tpu_custom_call" | custom-call | tf_op jit(solution)/shard_map/attend/pallas_call | solution.py:581
  68.7 1.3 fusion.21
  69.9 1.3 add_convert_fusion
  71.2 1.1 convolution_convert_fusion.1
  72.4 1.1 convolution_convert_fusion
  73.5 46.9 %sum_back.1 = (bf16[32,16,896]{2,1,0:T(8,128)(2,1)S(1)}, f32[112,2,1024]{2,1,0:T(2,128)S(1)}) custom-call(bf16[32,16,896]{2,1,0:T(8,128)(2,1)S(1)} %bitcast.58, bf16[8,112,1024]{2,1,0:T(8,128)(2,1)S(1)} %bitcast.50, bf16[8,112,1024]{2,1,0:T(8,128)(2,1)S(1)} %bitcast.52), custom_call_target="tpu_custom_call" | custom-call | tf_op jit(solution)/shard_map/sum_back/pallas_call | solution.py:490
  120.5 1.2 fusion.5
  121.7 1.1 convolution_convert_fusion.2
  122.9 1.1 convolution_convert_fusion.3
  124.0 17.6 %sum_grads.1 = (f32[112,896]{1,0:T(8,128)S(1)}, f32[112,896]{1,0:T(8,128)S(1)}) custom-call(bf16[8,112,896]{2,1,0:T(8,128)(2,1)S(1)} %bitcast.54, bf16[8,112,896]{2,1,0:T(8,128)(2,1)S(1)} %bitcast.53), custom_call_target="tpu_custom_call" | custom-call | tf_op jit(solution)/shard_map/sum_grads/pallas_call | solution.py:524
  141.6 0.9 copy.23
  142.6 0.7 copy.24
  143.3 0.7 copy.25
  (9 shorter events, 0.1 us)
Async XLA Ops:
  0.6 26.5 %copy-start = (bf16[896,896]{1,0:T(8,128)(2,1)S(1)}, bf16[896,896]{1,0:T(8,128)(2,1)}, u32[]{:S(2)}) copy-start(bf16[896,896]{1,0:T(8,128)(2,1)} %param.12) | copy-start | bytes 4816900
  3.5 2.3 %copy-start.1 = (bf16[896,2,1024]{2,1,0:T(2,128)(2,1)S(1)}, bf16[896,2,1024]{2,1,0:T(2,128)(2,1)}, u32[]{:S(2)}) copy-start(bf16[896,2,1024]{2,1,0:T(2,128)(2,1)} %pairs.1) | copy-start | bytes 11010052
  27.2 1.4 copy-start.4
  64.3 1.3 copy-start.2
  64.4 1.3 copy-start.3

commit v7 on v6

--- a/solution.py
+++ b/solution.py
@@ -12,10 +12,8 @@
 NEIGH = 2
 TAG_ROWS = 16
 LANES = 128
-CHAIN_CHUNKS = 32
-ROOT_LAG = 6
-CHAIN_LAG = 12
-CHAIN_WINDOW = 8
+ENCODED_CHUNKS = 32
+BACK_CHUNKS = 16
 HEADS_AT_ONCE = 4
 VMEM_BYTES = 24 * 1024 * 1024
 
@@ -82,7 +80,10 @@
         self.me = lax.axis_index("mp")
         self.chunks = part.shape[0]
         self.is_end = jnp.logical_or(self.me == 0, self.me == size - 1)
-        self.steps = self.chunks + CHAIN_LAG
+        self.root_lag = 2 + self.chunks // 8
+        self.lag = 2 * self.root_lag
+        self.window = self.chunks // 4
+        self.steps = self.chunks + self.lag
 
     def root(self, chunk):
         return self.size // 2 - 1 + chunk % 2
@@ -146,8 +147,8 @@
 
             @pl.when(here)
             def _(toward=toward):
-                if chunk >= CHAIN_WINDOW:
-                    self.up(chunk - CHAIN_WINDOW, toward, self.part).wait_send()
+                if chunk >= self.window:
+                    self.up(chunk - self.window, toward, self.part).wait_send()
                 self.up(chunk, toward, self.part).start()
 
     def step(self, index):
@@ -160,10 +161,10 @@
         def _():
             if index < self.chunks:
                 self.inner_up(index)
-            if 0 <= index - ROOT_LAG < self.chunks:
-                self.inner_root(index - ROOT_LAG)
-            if index >= CHAIN_LAG:
-                self.inner_down(index - CHAIN_LAG)
+            if 0 <= index - self.root_lag < self.chunks:
+                self.inner_root(index - self.root_lag)
+            if index >= self.lag:
+                self.inner_down(index - self.lag)
 
     def finish(self):
         for toward, here in ((1, self.me == 0), (-1, self.me == self.size - 1)):
@@ -172,7 +173,7 @@
             def _(toward=toward):
                 for chunk in range(self.chunks):
                     self.outward(chunk, toward).wait_recv()
-                for chunk in range(self.chunks - CHAIN_WINDOW, self.chunks):
+                for chunk in range(self.chunks - self.window, self.chunks):
                     self.up(chunk, toward, self.part).wait_send()
 
         @pl.when(jnp.logical_not(self.is_end))
@@ -626,11 +627,11 @@
     hidden_pre = jnp.dot(normed, in_weight, preferred_element_type=jnp.float32)
     activated = lax.optimization_barrier(gelu_value(hidden_pre).astype(jnp.bfloat16))
     part = jnp.dot(activated, out_weight, preferred_element_type=jnp.float32).astype(jnp.bfloat16)
-    sliced = (CHAIN_CHUNKS, tokens // CHAIN_CHUNKS, width)
+    sliced = (ENCODED_CHUNKS, tokens // ENCODED_CHUNKS, width)
     encoded, slope = sum_over_mp(
         part.reshape(sliced),
         raw.reshape(sliced),
-        hidden_pre.reshape(CHAIN_CHUNKS, tokens // CHAIN_CHUNKS, -1),
+        hidden_pre.reshape(ENCODED_CHUNKS, tokens // ENCODED_CHUNKS, -1),
         n_mp,
     )
     encoded = encoded.reshape(tokens, width)
@@ -648,7 +649,7 @@
     key_terms = matmul(encoded, d_keys, 0, 0).astype(jnp.bfloat16).reshape(chunked)
     value_terms = matmul(encoded, d_values, 0, 0).astype(jnp.bfloat16).reshape(chunked)
     d_encoded, grad_kv = back_sums(
-        back.reshape(sliced), key_terms, value_terms, n_mp, n_dp
+        back.reshape(BACK_CHUNKS, tokens // BACK_CHUNKS, width), key_terms, value_terms, n_mp, n_dp
     )
     d_encoded = d_encoded.reshape(tokens, width)
 

time: 144 us -> 136 us (0.944)
  Pallas kernels: 122 us -> 113 us
    pallas_call x1, Pallas kernels: 46.9 us -> 38.6 us  [back_sums(): pl.pallas_call(functools.partial(back_kernel, n_mp, n_dp), out_shape=(jax...]
where the time goes in v7:
time: 136 us
  Pallas kernels  113 us (83%)
  matrix products  16.3 us (12%)
  local copies, waits for them, and re-layouts  3.14 us (2%)
  between operations  1.62 us (1%)
    pallas_call x1, Pallas kernels, back_sums(): pl.pallas_call(functools.partial(back_kernel, n_mp, n_dp), out_shape=(jax...  38.6 us
    pallas_call x1, Pallas kernels, sum_over_mp(): pl.pallas_call(functools.partial(sum_kernel, n_mp), out_shape=(jax.ShapeD...  33.3 us
    pallas_call x1, Pallas kernels, route(): pl.pallas_call(functools.partial(route_kernel, n_dp, n_mp, straight, spli...  20.9 us
    pallas_call x1, Pallas kernels, grad_sums(): pl.pallas_call(functools.partial(grads_kernel, n_dp), out_shape=(jax.Shap...  17.5 us
    dot_general x7, matrix products, matmul(): lax.dot_general(left, right, (((left_dim,), (right_dim,)), ((), ())), pre...  8.38 us
    pallas_call x1, Pallas kernels, attend(): pl.pallas_call(functools.partial(attend_kernel, spans), out_shape=(small,...  3 us
    unnamed x13, local copies, waits for them, and re-layouts  2.9 us
    dot_general x2, matrix products, picked(): jnp.einsum('oh,thd->otd', picks, rows, preferred_element_type=jnp.float32)  2.86 us

profile of v7, /device:TPU:0, one launch (start us, length us, event | category | flops | bytes accessed | tf_op | source)
XLA Modules:
  0.0 135.6 jit_solution(1760655249255845089)
XLA Ops:
  0.6 0.0 copy-start
  1.4 0.7 and_select_fusion.1
  2.1 0.1 select_reduce_fusion
  2.2 0.1 broadcast_in_dim.16.refs_0_
  2.3 1.1 fusion.9
  3.5 1.7 %fusion.7 = bf16[8,64,896]{2,0,1:T(8,128)(2,1)S(1)} fusion(bf16[128,8,896]{2,1,0:T(8,128)(2,1)} %param.9, s32[8]{0:T(128)S(1)} %get-tuple-element.31, pred[8]{0:T(512)(128)(4,1)S(1)} %iota_compare_fusion.1), kind=kOutput, calls=%fused_computation.20 | convolution fusion | flops 7340160 | bytes 1835048 | tf_op jit(solution)/shard_map/oh,thd->otd/dot_general | solution.py:606
  5.2 0.1 copy.17.refs_2_
  5.4 0.4 copy-done.1
  5.8 20.9 %route.1 = (bf16[4,128,896]{2,1,0:T(8,128)(2,1)S(1)}, bf16[896,1024]{1,0:T(8,128)(2,1)S(1)}, bf16[896,1024]{1,0:T(8,128)(2,1)S(1)}) custom-call(bf16[896,2,1024]{2,1,0:T(2,128)(2,1)S(1)} %copy-done.1, bf16[8,16,128]{2,1,0:T(8,128)(2,1)S(1)} %broadcast_in_dim.16.refs_0_, bf16[8,16,896]{2,1,0:T(8,128)(2,1)S(1)} %copy.18.refs_1_, ...), custom_call_target="tpu_custom_call" | custom-call | tf_op jit(solution)/shard_map/route/pallas_call | solution.py:409
  26.7 0.3 multiply_reduce_fusion
  26.9 0.2 fusion.6
  27.2 0.0 copy-start.4
  27.2 1.4 %fusion.4 = (bf16[512,896]{1,0:T(8,128)(2,1)S(1)}, f32[512,896]{1,0:T(8,128)S(1)}) fusion(bf16[512,896]{1,0:T(8,128)(2,1)S(1)} %fusion.6, bf16[896,896]{1,0:T(8,128)(2,1)S(1)} %copy-done), kind=kOutput, calls=%fused_computation.5 | convolution fusion | flops 826212352 | bytes 5275648 | tf_op jit(solution)/shard_map/dot_general | solution.py:627
  28.6 0.0 copy-done.4
  28.6 1.2 convolution_convert_fusion.6
  29.8 33.3 %sum_encoded.1 = (bf16[32,16,896]{2,1,0:T(8,128)(2,1)S(1)}, f32[32,16,896]{2,1,0:T(8,128)S(1)}) custom-call(bf16[32,16,896]{2,1,0:T(8,128)(2,1)S(1)} %bitcast.57, bf16[32,16,896]{2,1,0:T(8,128)(2,1)S(1)} %bitcast.49, f32[32,16,896]{2,1,0:T(8,128)S(1)} %bitcast.51), custom_call_target="tpu_custom_call" | custom-call | tf_op jit(solution)/shard_map/sum_encoded/pallas_call | solution.py:446
  63.1 1.3 convolution_convert_fusion.4.values
  64.4 0.0 copy-start.3
  64.4 1.3 convolution_convert_fusion.5.keys
  65.7 3.0 %attend.1 = (bf16[128,1024]{1,0:T(8,128)(2,1)}, bf16[128,1024]{1,0:T(8,128)(2,1)}, bf16[512,1024]{1,0:T(8,128)(2,1)S(1)}, bf16[512,1024]{1,0:T(8,128)(2,1)S(1)}) custom-call(bf16[128,1024]{1,0:T(8,128)(2,1)S(1)} %copy-done.2, bf16[512,1024]{1,0:T(8,128)(2,1)S(1)} %convolution_convert_fusion.5.keys, bf16[512,1024]{1,0:T(8,128)(2,1)S(1)} %convolution_convert_fusion.4.values, ...), custom_call_target="tpu_custom_call" | custom-call | tf_op jit(solution)/shard_map/attend/pallas_call | solution.py:582
  68.7 1.3 fusion.21
  69.9 1.3 add_convert_fusion
  71.2 1.1 convolution_convert_fusion.1
  72.4 1.1 convolution_convert_fusion
  73.5 38.6 %sum_back.1 = (bf16[16,32,896]{2,1,0:T(8,128)(2,1)S(1)}, f32[112,2,1024]{2,1,0:T(2,128)S(1)}) custom-call(bf16[16,32,896]{2,1,0:T(8,128)(2,1)S(1)} %bitcast.58, bf16[8,112,1024]{2,1,0:T(8,128)(2,1)S(1)} %bitcast.50, bf16[8,112,1024]{2,1,0:T(8,128)(2,1)S(1)} %bitcast.52), custom_call_target="tpu_custom_call" | custom-call | tf_op jit(solution)/shard_map/sum_back/pallas_call | solution.py:491
  112.1 1.2 fusion.5
  113.3 1.1 convolution_convert_fusion.2
  114.5 1.1 convolution_convert_fusion.3
  115.6 17.5 %sum_grads.1 = (f32[112,896]{1,0:T(8,128)S(1)}, f32[112,896]{1,0:T(8,128)S(1)}) custom-call(bf16[8,112,896]{2,1,0:T(8,128)(2,1)S(1)} %bitcast.54, bf16[8,112,896]{2,1,0:T(8,128)(2,1)S(1)} %bitcast.53), custom_call_target="tpu_custom_call" | custom-call | tf_op jit(solution)/shard_map/sum_grads/pallas_call | solution.py:525
  133.2 0.9 copy.23
  134.1 0.7 copy.24
  134.8 0.7 copy.25
  (9 shorter events, 0.1 us)
Async XLA Ops:
  0.6 26.5 %copy-start = (bf16[896,896]{1,0:T(8,128)(2,1)S(1)}, bf16[896,896]{1,0:T(8,128)(2,1)}, u32[]{:S(2)}) copy-start(bf16[896,896]{1,0:T(8,128)(2,1)} %param.12) | copy-start | bytes 4816900
  3.5 2.3 %copy-start.1 = (bf16[896,2,1024]{2,1,0:T(2,128)(2,1)S(1)}, bf16[896,2,1024]{2,1,0:T(2,128)(2,1)}, u32[]{:S(2)}) copy-start(bf16[896,2,1024]{2,1,0:T(2,128)(2,1)} %pairs.1) | copy-start | bytes 11010052
  27.2 1.4 %copy-start.4 = (bf16[896,896]{1,0:T(8,128)(2,1)S(1)}, bf16[896,896]{1,0:T(8,128)(2,1)}, u32[]{:S(2)}) copy-start(bf16[896,896]{1,0:T(8,128)(2,1)} %param.13) | copy-start | bytes 4816900
  64.3 1.3 copy-start.2
  64.4 1.3 copy-start.3
